TPU v7x, 256 devices: a whole 4x4x8 slice. The times are simulated.
256 devices in a mesh: stn: 64 (over z_hi, x, y), beam: 4 (over z_lo, core).
Axes of the slice: x: 4, y: 4, z: 8 (z_hi: 4, z_lo: 2; z = z_hi * 2 + z_lo), core: 2. Of those that a mesh axis runs over, the one named last changes fastest.
Arguments:
- voltages: bfloat16 [2, 1024, 131072], P(None, 'stn', 'beam'), may hold values from -6 to 6
- filter_taps: float32 [12, 128], replicated, may hold values from -1.8 to 1.8
- synth_taps: float32 [12, 128], replicated, may hold values from -1.8 to 1.8
- beam_weights: bfloat16 [2, 128, 512, 1024], P(None, 'stn', 'beam'), may hold values from -0.125 to 0.125
- station_order: int32 [1024], replicated, may hold values from 0 to 1023, each once
Outputs:
- visibilities: float32 [2, 128, 1024, 1024], P(None, 'stn', 'beam')
- beam_series: float32 [2, 4, 128, 131072], P(None, 'beam', 'stn')
Inputs may be any that keep to these rules, and one draw needn't show every extreme that they name: `station_order`: a permutation of the 1024 station numbers.
All inputs are finite; a program needn't handle non-finite values.
Results may differ from a plain program's by a relative error of at most 0.0029.
Values may be sent and summed in bfloat16 or wider, within the bound.
A program may use at most 128 MiB of HBM per device.

v0:
```python
import math

import jax
import jax.numpy as jnp
from jax import lax
from jax.sharding import PartitionSpec as P


def from_behind(block, axis, distance):
    devices = range(lax.axis_size(axis))
    route = [(i - distance, i) for i in devices if i - distance in devices]
    return lax.ppermute(block, axis, route)


def spin_matrix(points):
    positions = jnp.arange(points, dtype=jnp.int32)
    phase_idx = positions[:, None] * positions[None, :] % points
    angles = phase_idx.astype(jnp.float32) * (2.0 * math.pi / points)
    cosine = jnp.cos(angles) / math.sqrt(points)
    sine_part = jnp.sin(angles) / math.sqrt(points)
    upper_half = jnp.concatenate([cosine, -sine_part], axis=1)
    lower_half = jnp.concatenate([sine_part, cosine], axis=1)
    return jnp.concatenate([upper_half, lower_half], axis=0)


def local(voltages, filter_taps, synth_taps, beam_weights, station_order):
    beam_count = lax.axis_size("beam")
    tap_count = filter_taps.shape[0]
    channels = filter_taps.shape[1]
    local_stations = voltages.shape[1]
    spec_local = voltages.shape[2] // channels
    spectra = spec_local * beam_count
    stations = station_order.shape[0]
    group_beams = beam_weights.shape[2]
    matrix = spin_matrix(channels)
    rim_length = (tap_count - 1) * channels
    history = from_behind(voltages[:, :, voltages.shape[2] - rim_length :], "beam", 1)
    extended = jnp.concatenate([history, voltages], axis=2)
    extended = extended.reshape(2, local_stations, spec_local + tap_count - 1, channels)
    reordered = jnp.transpose(extended, (0, 3, 1, 2)).astype(jnp.float32)
    windowed = jnp.zeros((2, channels, local_stations, spec_local), jnp.float32)
    for tap_index in range(tap_count):
        begin_at = tap_count - 1 - tap_index
        windowed = (
            windowed
            + filter_taps[tap_index][None, :, None, None]
            * reordered[..., begin_at : begin_at + spec_local]
        )
    flattened = windowed.reshape(2 * channels, local_stations * spec_local)
    spectral = jnp.dot(
        matrix.T, flattened, precision=lax.Precision.HIGHEST, preferred_element_type=jnp.float32
    ).astype(jnp.bfloat16)
    spectral = spectral.reshape(2, channels, local_stations, spec_local)
    channel_data = lax.all_to_all(spectral, "stn", split_axis=1, concat_axis=2, tiled=True)
    inverse = (
        jnp.zeros((stations,), jnp.int32)
        .at[station_order]
        .set(jnp.arange(stations, dtype=jnp.int32))
    )
    channel_data = jnp.take(channel_data, inverse, axis=2)
    channel_local = channel_data.shape[1]
    row_count = stations // beam_count
    row_start = lax.axis_index("beam") * row_count
    weight_real = beam_weights[0]
    weight_imag = beam_weights[1]
    weights_wide = jnp.concatenate(
        [
            jnp.concatenate([weight_real, -weight_imag], axis=2),
            jnp.concatenate([weight_imag, weight_real], axis=2),
        ],
        axis=1,
    )
    pair_dims = (((2,), (2,)), ((0,), (0,)))
    beam_dims = (((2,), (1,)), ((0,), (0,)))
    fragment = lax.all_gather(channel_data, "beam", axis=3, tiled=True)
    joined = jnp.concatenate([fragment[0], fragment[1]], axis=2)
    rows_real = lax.dynamic_slice_in_dim(fragment[0], row_start, row_count, 1)
    rows_imag = lax.dynamic_slice_in_dim(fragment[1], row_start, row_count, 1)
    rows_joined = jnp.concatenate([rows_real, rows_imag], axis=2)
    rows_turned = jnp.concatenate([rows_imag, -rows_real], axis=2)
    real_part = lax.dot_general(rows_joined, joined, pair_dims, preferred_element_type=jnp.float32)
    imag_part = lax.dot_general(rows_turned, joined, pair_dims, preferred_element_type=jnp.float32)
    real_part, imag_part = (real_part, imag_part)
    fragment = lax.all_gather(channel_data, "beam", axis=3, tiled=True)
    stacked = jnp.concatenate([fragment[0], fragment[1]], axis=1)
    formed = lax.dot_general(weights_wide, stacked, beam_dims, preferred_element_type=jnp.float32)
    visibilities = jnp.stack([real_part, imag_part]) / spectra
    formed = formed.reshape(channel_local, 2, group_beams, spectra)
    arrived = lax.all_to_all(formed, "stn", split_axis=2, concat_axis=0, tiled=True)
    local_beams = arrived.shape[2]
    arranged = jnp.transpose(arrived, (1, 0, 2, 3)).reshape(2 * channels, local_beams * spectra)
    resynth = jnp.dot(
        matrix, arranged, precision=lax.Precision.HIGHEST, preferred_element_type=jnp.float32
    )
    resynth = resynth.reshape(2, channels, local_beams, spectra)
    padded_series = jnp.pad(resynth, ((0, 0), (0, 0), (0, 0), (tap_count - 1, 0)))
    series = jnp.zeros_like(resynth)
    for tap_index in range(tap_count):
        begin_at = tap_count - 1 - tap_index
        series = (
            series
            + synth_taps[tap_index][None, :, None, None]
            * padded_series[..., begin_at : begin_at + spectra]
        )
    series = jnp.transpose(series, (0, 2, 3, 1)).reshape(2, 1, local_beams, spectra * channels)
    return (visibilities, series)


def solution(mesh):
    in_specs = (P(None, "stn", "beam"), P(), P(), P(None, "stn", "beam", None), P())
    out_specs = (P(None, "stn", "beam", None), P(None, "beam", "stn", None))
    return jax.shard_map(local, mesh=mesh, in_specs=in_specs, out_specs=out_specs, check_vma=False)
```

profile of v0, /device:TPU:1, one launch (start us, length us, event | category | flops | bytes accessed | tf_op | source)
XLA Modules:
  0.0 325.6 jit_solution(12021670346092727932)
XLA Ops:
  8.1 4.9 %collective-permute-start = (bf16[2,16,1408]{2,1,0:T(8,128)(2,1)S(1)}, bf16[2,16,1408]{2,1,0:T(8,128)(2,1)S(1)}, u32[]{:S(2)}, u32[]{:S(2)}) collective-permute-start(bf16[2,16,1408]{2,1,0:T(8,128)(2,1)S(1)} %slice.162), channel_id=1, source_target_pairs={{0,1},{1,2},{2,3},{4,5},{5,6},{6,7},{8,9},{9,10},{10,11},{12,13},{... | collective-permute-start | bytes 270344 | tf_op jit(solution)/shard_map/ppermute | solution.py:12
  14.6 3.9 %maximum_convert_fusion = f32[2,16,34176]{2,1,0:T(8,128)} fusion(bf16[2,16,32768]{2,1,0:T(8,128)(2,1)} %param.5, bf16[2,16,1408]{2,1,0:T(8,128)(2,1)S(1)} %collective-permute-done), kind=kLoop, calls=%fused_computation.45 | loop fusion | flops 4374528 | bytes 6561792 | tf_op jit(solution)/shard_map/convert_element_type | solution.py:40
  18.5 5.0 %reshape.61 = f32[2,16,267,128]{3,2,1,0:T(8,128)} reshape(f32[2,16,34176]{2,1,0:T(8,128)} %maximum_convert_fusion) | data formatting | bytes 8749056 | tf_op jit(solution)/shard_map/convert_element_type | solution.py:40
  23.5 22.4 %fusion.6 = f32[2,128,16,256]{1,3,2,0:T(8,128)} fusion(f32[2,128,16,267]{1,3,2,0:T(8,128)} %bitcast.108, f32[128]{0:T(128)S(1)} %get-tuple-element.38, f32[128]{0:T(128)S(1)} %get-tuple-element.39, f32[128]{0:T(128)S(1)} %get-tuple-element.29, f32[128]{0:T(128)S(1)} %get-tuple-element.30, f32[128]{0:T(128)S(1)} %get-tuple-element.31, ...), kind=kLoop, calls=%fused_computation.11 | loop fusion | flops 24117248 | bytes 54532096 | tf_op jit(solution)/shard_map/add | solution.py:45
  45.9 5.5 %copy.22 = f32[2,128,16,256]{3,2,1,0:T(8,128)} copy(f32[2,128,16,256]{1,3,2,0:T(8,128)} %fusion.6) | data formatting | bytes 8388608 | tf_op jit(solution)/shard_map/add | solution.py:45
  51.4 6.0 %copy.38 = f32[32,8,16,256]{3,1,2,0:T(8,128)S(1)} copy(f32[32,8,16,256]{3,2,1,0:T(8,128)} %bitcast.110) | data formatting | bytes 8388608
  57.3 3.8 %convolution_convert_fusion = bf16[256,4096]{1,0:T(8,128)(2,1)S(1)} fusion(f32[256,4096]{1,0:T(8,128)S(1)} %bitcast.109, f32[128,128]{1,0:T(8,128)S(1)} %get-tuple-element.41, f32[128,128]{1,0:T(8,128)S(1)} %get-tuple-element.40, f32[128,128]{1,0:T(8,128)S(1)} %fusion.66), kind=kOutput, calls=%fused_computation.9 | convolution fusion | flops 3222470656 | bytes 6488064 | tf_op jit(solution)/shard_map/dot_general | solution.py:50
  63.5 13.4 %all-to-all-start = ((bf16[2,128,16,256]{3,2,0,1:T(8,128)(2,1)}), bf16[2,128,16,256]{3,2,0,1:T(8,128)(2,1)S(1)}, u32[]{:S(2)}, u32[]{:S(2)}) async-start(bf16[2,128,16,256]{3,2,0,1:T(8,128)(2,1)} %copy.23), calls=%async_computation | async-start | bytes 4194304 | tf_op jit(solution)/shard_map/all_to_all | solution.py:54
  77.0 4.3 %scatter_custom_fusion = s32[1024]{0:T(1024)S(1)} fusion(s32[1024]{0:T(1024)S(1)} %compare_select_fusion.1, s32[1024]{0:T(1024)S(1)} %iota.10, s32[]{:T(128)} %constant.41.clone.1), kind=kCustom, calls=%fused_computation.107 | custom fusion | bytes 4100 | tf_op jit(solution)/shard_map/scatter | solution.py:58
  81.3 47.5 %all-to-all-done = bf16[2,128,16,256]{3,2,0,1:T(8,128)(2,1)S(1)} async-done(((bf16[2,128,16,256]{3,2,0,1:T(8,128)(2,1)}), bf16[2,128,16,256]{3,2,0,1:T(8,128)(2,1)S(1)}, u32[]{:S(2)}, u32[]{:S(2)}) %all-to-all-start) | async-done | bytes 2097184 | tf_op jit(solution)/shard_map/all_to_all | solution.py:54
  129.0 3.5 %copy.26 = bf16[2,2,1024,256]{3,1,2,0:T(2,128)(2,1)} copy(bf16[2,2,1024,256]{3,2,1,0:T(8,128)(2,1)S(1)} %bitcast.116) | data formatting | bytes 4194304 | tf_op jit(solution)/shard_map/all_to_all | solution.py:54
  132.5 8.2 %gather_fusion = bf16[1024,2,2,256]{3,2,1,0:T(2,128)(2,1)S(1)} fusion(bf16[2,2,1024,256]{3,1,2,0:T(2,128)(2,1)} %copy.26, s32[1024]{0:T(1024)S(1)} %fusion.67), kind=kCustom, calls=%fused_computation | custom fusion | bytes 4198400 | tf_op jit(solution)/shard_map/jit(_take)/gather | solution.py:60
  142.5 80.5 %all-gather.2.cloned.1.call-done = bf16[2,2,1024,1024]{3,2,1,0:T(8,128)(2,1)} async-done(((bf16[2,2,1024,256]{3,2,1,0:T(8,128)(2,1)}), bf16[2,2,1024,1024]{3,2,1,0:T(8,128)(2,1)}) %all-gather.2.cloned.1.call-update) | async-done | bytes 8388624 | tf_op jit(solution)/shard_map/all_gather | solution.py:75
  223.0 6.1 %fusion.75 = (bf16[1,2,1024,1024]{3,2,1,0:T(8,128)(2,1)}, bf16[2,1024,1024]{2,1,0:T(8,128)(2,1)S(1)}, bf16[2,1024,1024]{2,1,0:T(8,128)(2,1)S(1)}, bf16[1,2,1024,1024]{3,2,1,0:T(8,128)(2,1)}) fusion(bf16[2,2,1024,1024]{3,2,1,0:T(8,128)(2,1)} %all-gather.2.cloned.1.call-done), kind=kLoop, calls=%fused_computation.140 | loop fusion | bytes 25165824 | tf_op jit(solution)/shard_map/slice | solution.py:78
  229.2 2.6 fusion
  232.4 2.9 copy.28
  235.3 11.9 %all-to-all-start.1 = ((f32[2,2,128,1024]{3,1,0,2:T(2,128)}), f32[2,2,128,1024]{3,1,0,2:T(2,128)S(1)}, u32[]{:S(2)}, u32[]{:S(2)}) async-start(f32[2,2,128,1024]{3,1,0,2:T(2,128)} %copy.28), calls=%async_computation.1 | async-start | bytes 4194304 | tf_op jit(solution)/shard_map/all_to_all | solution.py:89
  248.8 2.6 fusion.74
  251.4 4.4 %fusion.54 = f32[1,2,256,1024]{3,2,1,0:T(8,128)S(1)} fusion(bf16[2,1024,1024]{2,1,0:T(8,128)(2,1)} %copy-done.2, bf16[2,1024,1024]{2,1,0:T(8,128)(2,1)S(1)} %copy-done.1, bf16[2,256,1024]{2,1,0:T(8,128)(2,1)S(1)} %dynamic-slice_bitcast_fusion, bf16[2,256,1024]{2,1,0:T(8,128)(2,1)S(1)} %get-tuple-element.9), kind=kOutput, calls=%fused_computation.84 | convolution fusion | flops 2168455168 | bytes 12582912 | tf_op jit(solution)/shard_map/dot_general | solution.py:81
  255.8 3.7 %fusion.57 = f32[1,2,256,1024]{3,2,1,0:T(8,128)S(1)} fusion(bf16[2,1024,1024]{2,1,0:T(8,128)(2,1)S(1)} %copy-done.3, bf16[2,1024,1024]{2,1,0:T(8,128)(2,1)S(1)} %copy-done.1, bf16[2,256,1024]{2,1,0:T(8,128)(2,1)} %get-tuple-element.8, bf16[2,256,1024]{2,1,0:T(8,128)(2,1)S(1)} %dynamic-slice_bitcast_fusion), kind=kOutput, calls=%fused_computation.85 | convolution fusion | flops 2168455168 | bytes 12582912 | tf_op jit(solution)/shard_map/dot_general | solution.py:82
  259.5 2.5 maximum_multiply_fusion
  262.0 35.9 %all-to-all-done.1 = f32[2,2,128,1024]{3,1,0,2:T(2,128)S(1)} async-done(((f32[2,2,128,1024]{3,1,0,2:T(2,128)}), f32[2,2,128,1024]{3,1,0,2:T(2,128)S(1)}, u32[]{:S(2)}, u32[]{:S(2)}) %all-to-all-start.1) | async-done | bytes 2097184 | tf_op jit(solution)/shard_map/all_to_all | solution.py:89
  306.6 6.7 %fusion.29 = f32[2,2,1024,128]{2,3,1,0:T(8,128)S(1)} fusion(f32[2,128,2,1024]{3,1,2,0:T(8,128)S(1)} %fusion.76, f32[128]{0:T(128)S(1)} %get-tuple-element.26, f32[128]{0:T(128)S(1)} %get-tuple-element.27, f32[128]{0:T(128)S(1)} %get-tuple-element.17, f32[128]{0:T(128)S(1)} %get-tuple-element.18, f32[128]{0:T(128)S(1)} %get-tuple-element.19, ...), kind=kLoop, calls=%fused_computation.58 | loop fusion | flops 12058624 | bytes 4200448 | tf_op jit(solution)/shard_map/transpose | solution.py:105
  315.2 3.5 %reshape.60 = f32[2,1,2,131072]{3,2,0,1:T(2,128)} reshape(f32[2,2,1024,128]{3,2,1,0:T(8,128)} %copy.33) | data formatting | bytes 4194304 | tf_op jit(solution)/shard_map/reshape | solution.py:105
  (40 shorter events, 19.4 us)
Async XLA Ops:
  8.1 6.5 %collective-permute-start = (bf16[2,16,1408]{2,1,0:T(8,128)(2,1)S(1)}, bf16[2,16,1408]{2,1,0:T(8,128)(2,1)S(1)}, u32[]{:S(2)}, u32[]{:S(2)}) collective-permute-start(bf16[2,16,1408]{2,1,0:T(8,128)(2,1)S(1)} %slice.162), channel_id=1, source_target_pairs={{0,1},{1,2},{2,3},{4,5},{5,6},{6,7},{8,9},{9,10},{10,11},{12,13},{... | collective-permute-start | bytes 270344 | tf_op jit(solution)/shard_map/ppermute | solution.py:12
  61.8 15.1 %copy-start.6 = (s32[1024]{0:T(1024)S(1)}, s32[1024]{0:T(1024)}, u32[]{:S(2)}) copy-start(s32[1024]{0:T(1024)} %param.9) | copy-start | bytes 12292
  63.5 65.3 %all-to-all-start = ((bf16[2,128,16,256]{3,2,0,1:T(8,128)(2,1)}), bf16[2,128,16,256]{3,2,0,1:T(8,128)(2,1)S(1)}, u32[]{:S(2)}, u32[]{:S(2)}) async-start(bf16[2,128,16,256]{3,2,0,1:T(8,128)(2,1)} %copy.23), calls=%async_computation | async-start | bytes 4194304 | tf_op jit(solution)/shard_map/all_to_all | solution.py:54
  76.9 146.2 %all-gather.2.cloned.1.call-start = ((), (), s32[]{:S(2)}) async-start(), calls=%async_computation.2 | async-start | bytes 10485760 | tf_op jit(solution)/shard_map/all_gather | solution.py:75
  140.7 1.7 copy-start.4
  229.2 2.6 copy-start
  229.2 3.2 copy-start.2
  232.4 14.9 %copy-start.5 = (f32[12,128]{1,0:T(8,128)S(1)}, f32[12,128]{1,0:T(8,128)}, u32[]{:S(2)}) copy-start(f32[12,128]{1,0:T(8,128)} %param.7) | copy-start | bytes 18436
  235.3 62.5 %all-to-all-start.1 = ((f32[2,2,128,1024]{3,1,0,2:T(2,128)}), f32[2,2,128,1024]{3,1,0,2:T(2,128)S(1)}, u32[]{:S(2)}, u32[]{:S(2)}) async-start(f32[2,2,128,1024]{3,1,0,2:T(2,128)} %copy.28), calls=%async_computation.1 | async-start | bytes 4194304 | tf_op jit(solution)/shard_map/all_to_all | solution.py:89
  247.3 4.1 %copy-start.1 = (bf16[2,1024,1024]{2,1,0:T(8,128)(2,1)S(1)}, bf16[2,1024,1024]{2,1,0:T(8,128)(2,1)}, u32[]{:S(2)}) copy-start(bf16[2,1024,1024]{2,1,0:T(8,128)(2,1)} %copy-done) | copy-start | bytes 12582916
  251.4 4.5 %copy-start.3 = (bf16[2,1024,1024]{2,1,0:T(8,128)(2,1)S(1)}, bf16[2,1024,1024]{2,1,0:T(8,128)(2,1)}, u32[]{:S(2)}) copy-start(bf16[2,1024,1024]{2,1,0:T(8,128)(2,1)} %copy-done.2) | copy-start | bytes 12582916
Sparse Core Ops, SparseCore 0:
  142.5 80.4 all-gather.1
where the time goes:
time: 328 us; the launch traced here: 326 us
  waiting for transfers between devices  164 us (50%)
  local copies, waits for them, and re-layouts  60.3 us (18%)
  other arithmetic  40.4 us (12%)
  starting transfers between devices  30.3 us (9%)
  matrix products  16.5 us (5%)
  between operations  14.3 us (4%)
    all_gather x1, waiting for transfers between devices, local(): fragment = lax.all_gather(channel_data, 'beam', axis=3, tiled=True)  80.5 us
    all_to_all x1, waiting for transfers between devices, local(): lax.all_to_all(spectral, 'stn', split_axis=1, concat_axis=2, tiled=True)  47.5 us
    all_to_all x1, waiting for transfers between devices, local(): lax.all_to_all(formed, 'stn', split_axis=2, concat_axis=0, tiled=True)  35.9 us
    add x1, other arithmetic, local(): windowed + filter_taps[tap_index][None, :, None, None] * reordered[..., b...  22.4 us
    all_to_all x1, starting transfers between devices, local(): lax.all_to_all(spectral, 'stn', split_axis=1, concat_axis=2, tiled=True)  13.4 us
    all_to_all x1, starting transfers between devices, local(): lax.all_to_all(formed, 'stn', split_axis=2, concat_axis=0, tiled=True)  11.9 us
    unnamed x17, local copies, waits for them, and re-layouts  9.43 us
    gather x1, local copies, waits for them, and re-layouts, local(): channel_data = jnp.take(channel_data, inverse, axis=2)  8.23 us
  transfers between devices with their start and end apart: 4, of which 3 were waited for; matrix products, arithmetic and copies ran while one was open for 6% of the time, Pallas kernels for 0%

commit v1 on v0

v1 whole, which is shorter than its diff:
```python
import functools
import math

import jax
import jax.numpy as jnp
import numpy as np
from jax import lax
from jax.experimental import pallas as pl
from jax.experimental.pallas import tpu as pltpu
from jax.sharding import PartitionSpec as P

F32, BF16 = jnp.float32, jnp.bfloat16
MIB = 2**20


def spin_matrix(points):
    index = np.arange(points)
    angles = (index[:, None] * index[None, :] % points) * (2.0 * math.pi / points)
    cosine, sine = np.cos(angles) / math.sqrt(points), np.sin(angles) / math.sqrt(points)
    upper = np.concatenate([cosine, -sine], axis=1)
    lower = np.concatenate([sine, cosine], axis=1)
    return np.concatenate([upper, lower], axis=0).astype(np.float32)


def split(matrix):
    high = matrix.astype(jnp.bfloat16)
    low = (matrix - high.astype(np.float32)).astype(jnp.bfloat16)
    return jnp.asarray(high), jnp.asarray(low)


def dot(a, b, dims):
    return lax.dot_general(a, b, (dims, ((), ())), preferred_element_type=F32)


def front_kernel(taps, channels, v_ref, h_ref, taps_ref, high_ref, low_ref, out_ref, re_ref, im_ref, left_ref, right_ref):
    stations = v_ref.shape[1]
    spectra = v_ref.shape[2] // channels
    step = 8
    weights = [jnp.broadcast_to(taps_ref[m : m + 1, :], (stations, channels)) for m in range(taps)]

    def window(tile, t0, part, store):
        tiles = [tile(part, i - (taps - 1)) for i in range(step + taps - 1)]
        for j in range(step):
            total = weights[0] * tiles[j + taps - 1]
            for m in range(1, taps):
                total += weights[m] * tiles[j + taps - 1 - m]
            store[pl.ds((t0 + j) * stations, stations), :] = total

    for block in range(2):
        for part, store in ((0, re_ref), (1, im_ref)):

            def tile(part, i, block=block):
                t = block * step + i
                ref, at = (v_ref, t) if t >= 0 else (h_ref, t + taps - 1)
                return ref[part, :, at * channels : (at + 1) * channels].astype(F32)

            window(tile, block * step, part, store)

    @pl.loop(2, spectra // step)
    def _(block):
        for part, store in ((0, re_ref), (1, im_ref)):

            def tile(part, i):
                at = pl.multiple_of((block * step + i) * channels, channels)
                return v_ref[part, :, pl.ds(at, channels)].astype(F32)

            window(tile, block * step, part, store)

    rows = high_ref.shape[0]
    for s in range(stations):
        wide = jnp.concatenate(
            [re_ref[pl.ds(s, spectra, stride=stations), :], im_ref[pl.ds(s, spectra, stride=stations), :]], axis=1
        )
        high = wide.astype(BF16)
        low = (wide - high.astype(F32)).astype(BF16)
        nt = ((1,), (1,))
        result = dot(high_ref[...], high, nt) + dot(high_ref[...], low, nt) + dot(low_ref[...], high, nt)
        left_ref[pl.ds(s, rows, stride=stations), :] = result[:, :128]
        right_ref[pl.ds(s, rows, stride=stations), :] = result[:, 128:]

    @pl.loop(0, rows // 16)
    def _(i):
        at = pl.ds(i * 16 * stations, 16 * stations)
        out_ref[at, :128] = left_ref[at, :].astype(BF16)
        out_ref[at, 128:] = right_ref[at, :].astype(BF16)


def front(voltages, history, filter_taps):
    _, stations, samples = voltages.shape
    taps, channels = filter_taps.shape
    spectra = samples // channels
    order = np.array([ri * channels + c for c in range(channels) for ri in range(2)])
    high, low = split(spin_matrix(channels).T[order])
    vmem = pl.BlockSpec(memory_space=pltpu.VMEM)
    return pl.pallas_call(
        functools.partial(front_kernel, taps, channels),
        out_shape=jax.ShapeDtypeStruct((2 * channels * stations, spectra), BF16),
        in_specs=[vmem] * 5,
        out_specs=vmem,
        scratch_shapes=[pltpu.VMEM((spectra * stations, channels), F32)] * 2
        + [pltpu.VMEM((2 * channels * stations, 128), F32)] * 2,
        compiler_params=pltpu.CompilerParams(vmem_limit_bytes=40 * MIB),
        name="front",
    )(voltages, history, filter_taps, high, low)


def beams_kernel(quarters, w_ref, x_ref, out_ref, left_ref, right_ref):
    q = pl.program_id(1)
    groups = w_ref.shape[1] // 4
    stations = x_ref.shape[3]
    result = dot(w_ref[0, :, :stations], x_ref[0, 0, 0], ((1,), (0,)))
    result += dot(w_ref[0, :, stations:], x_ref[0, 0, 1], ((1,), (0,)))
    for i in range(4):
        rows = result[i * groups : (i + 1) * groups]
        left_ref[pl.ds(q * 4 + i, groups, stride=16), :] = rows[:, :128]
        right_ref[pl.ds(q * 4 + i, groups, stride=16), :] = rows[:, 128:]

    @pl.when(q == quarters - 1)
    def _():
        for d in range(0, groups, 8):
            at = slice(d * 16, (d + 8) * 16)
            out_ref[d : d + 8, 0, :, :128] = left_ref[at, :].astype(BF16).reshape(8, 16, 128)
            out_ref[d : d + 8, 0, :, 128:] = right_ref[at, :].astype(BF16).reshape(8, 16, 128)


def beams(weights, x):
    quarters, channels, _, stations, spectra = x.shape
    groups = weights.shape[1] // 4
    return pl.pallas_call(
        functools.partial(beams_kernel, quarters),
        grid=(channels, quarters),
        out_shape=jax.ShapeDtypeStruct((groups, channels, 16, spectra), BF16),
        in_specs=[
            pl.BlockSpec((1, 4 * groups, 2 * stations), lambda c, q: (c, 0, 0)),
            pl.BlockSpec((1, 1, 2, stations, spectra), lambda c, q: (q, c, 0, 0, 0)),
        ],
        out_specs=pl.BlockSpec((groups, 1, 16, spectra), lambda c, q: (0, c, 0, 0)),
        scratch_shapes=[pltpu.VMEM((groups * 16, 128), F32)] * 2,
        compiler_params=pltpu.CompilerParams(vmem_limit_bytes=40 * MIB),
        cost_estimate=pl.CostEstimate(flops=2 * 2**30, bytes_accessed=12 * MIB, transcendentals=0),
        name="beams",
    )(weights, x)


def pairs_kernel(scale, pick_ref, x_ref, out_ref, turned_ref, rows_ref):
    q = pl.program_id(1)
    stations = x_ref.shape[3]
    count = out_ref.shape[2]
    start = pl.multiple_of(lax.axis_index("beam") * count, count)
    for part in range(2):
        for r in range(0, stations, 256):
            turned_ref[part, r : r + 256, :] = dot(pick_ref[r : r + 256, :], x_ref[0, 0, part], ((1,), (0,))).astype(BF16)
        rows_ref[part] = turned_ref[part, pl.ds(start, count), :]
    nt = ((1,), (1,))
    for at in range(0, stations, 256):
        cols = slice(at, at + 256)
        real = dot(rows_ref[0], turned_ref[0, cols], nt) + dot(rows_ref[1], turned_ref[1, cols], nt)
        imag = dot(rows_ref[1], turned_ref[0, cols], nt) - dot(rows_ref[0], turned_ref[1, cols], nt)

        @pl.when(q == 0)
        def _():
            out_ref[0, 0, :, cols] = real * scale
            out_ref[1, 0, :, cols] = imag * scale

        @pl.when(q > 0)
        def _():
            out_ref[0, 0, :, cols] += real * scale
            out_ref[1, 0, :, cols] += imag * scale


def pairs(pick, x):
    quarters, channels, _, stations, spectra = x.shape
    return pl.pallas_call(
        functools.partial(pairs_kernel, 1.0 / (quarters * spectra)),
        grid=(channels, quarters),
        out_shape=jax.ShapeDtypeStruct((2, channels, stations // quarters, stations), F32),
        in_specs=[
            pl.BlockSpec((stations, stations), lambda c, q: (0, 0)),
            pl.BlockSpec((1, 1, 2, stations, spectra), lambda c, q: (q, c, 0, 0, 0)),
        ],
        out_specs=pl.BlockSpec((2, 1, stations // quarters, stations), lambda c, q: (0, c, 0, 0)),
        scratch_shapes=[pltpu.VMEM((2, stations, spectra), BF16), pltpu.VMEM((2, stations // quarters, spectra), BF16)],
        compiler_params=pltpu.CompilerParams(vmem_limit_bytes=40 * MIB),
        cost_estimate=pl.CostEstimate(flops=12 * 2**30, bytes_accessed=16 * MIB, transcendentals=0),
        name="pairs",
    )(pick, x)


def tail_kernel(taps, quarters, g_ref, taps_ref, high_ref, low_ref, out_ref, left_ref, right_ref, *lines):
    channels = high_ref.shape[0] // 2
    spectra = g_ref.shape[1]
    pad = 16
    left_ref[...] = g_ref[:, :128].astype(F32)
    right_ref[...] = g_ref[:, 128:].astype(F32)
    tn = ((0,), (0,))
    for line in lines:
        line[:pad, :] = jnp.zeros((pad, channels), F32)
    for j in range(2):
        for q in range(quarters):
            parts = [
                jnp.concatenate(
                    [ref[pl.ds(q * 4 + j * 2 + ri, channels, stride=16), :] for ref in (left_ref, right_ref)], axis=1
                )
                for ri in range(2)
            ]
            both = jnp.concatenate(parts, axis=0).astype(BF16)
            result = dot(both, high_ref[...], tn) + dot(both, low_ref[...], tn)
            at = slice(pad + q * spectra, pad + (q + 1) * spectra)
            lines[2 * j][at, :] = result[:, :channels]
            lines[2 * j + 1][at, :] = result[:, channels:]
    block = 64
    weights = [jnp.broadcast_to(taps_ref[m : m + 1, :], (block, channels)) for m in range(taps)]
    for j in range(2):
        for part in range(2):
            line = lines[2 * j + part]
            for t in range(0, quarters * spectra, block):
                total = weights[0] * line[pad + t : pad + t + block, :]
                for m in range(1, taps):
                    total += weights[m] * line[pad + t - m : pad + t - m + block, :]
                out_ref[part, pl.ds(2 * t + j, block, stride=2), :] = total


def tail(arrived, synth_taps, quarters):
    taps, channels = synth_taps.shape
    rows, spectra = arrived.shape
    high, low = split(spin_matrix(channels).T)
    vmem = pl.BlockSpec(memory_space=pltpu.VMEM)
    total = quarters * spectra
    return pl.pallas_call(
        functools.partial(tail_kernel, taps, quarters),
        out_shape=jax.ShapeDtypeStruct((2, 2 * total, channels), F32),
        in_specs=[vmem] * 4,
        out_specs=vmem,
        scratch_shapes=[pltpu.VMEM((rows, 128), F32)] * 2 + [pltpu.VMEM((total + 16, channels), F32)] * 4,
        compiler_params=pltpu.CompilerParams(vmem_limit_bytes=40 * MIB),
        name="tail",
    )(arrived, synth_taps, high, low)


def from_behind(block, axis, distance):
    devices = range(lax.axis_size(axis))
    route = [(i - distance, i) for i in devices if i - distance in devices]
    return lax.ppermute(block, axis, route)


def local(voltages, filter_taps, synth_taps, beam_weights, station_order):
    quarters = lax.axis_size("beam")
    owners = lax.axis_size("stn")
    taps, channels = filter_taps.shape
    rows = voltages.shape[1]
    spectra = voltages.shape[2] // channels
    stations = station_order.shape[0]
    held = channels // owners
    history = from_behind(voltages[:, :, voltages.shape[2] - (taps - 1) * channels :], "beam", 1)

    pick = (station_order[None, :] == jnp.arange(stations, dtype=jnp.int32)[:, None]).astype(BF16)
    turned = lax.dot_general(beam_weights, pick, (((3,), (0,)), ((), ())), preferred_element_type=F32).astype(BF16)
    turned = turned.reshape(2, held, owners, 2, stations).transpose(0, 1, 3, 2, 4)
    real_rows = jnp.concatenate([turned[0], -turned[1]], axis=-1)
    imag_rows = jnp.concatenate([turned[1], turned[0]], axis=-1)
    weights = jnp.stack([real_rows, imag_rows], axis=2).reshape(held, 4 * owners, 2 * stations)

    spectral = front(voltages, history, filter_taps).reshape(owners, held, 2, rows, spectra)
    mine = lax.all_to_all(spectral, "stn", split_axis=0, concat_axis=0, tiled=True)
    mine = mine.transpose(1, 2, 0, 3, 4).reshape(held, 2, stations, spectra)
    x = lax.all_gather(mine, "beam", axis=0, tiled=False)
    formed = beams(weights, x)
    arrived = lax.all_to_all(formed, "stn", split_axis=0, concat_axis=0, tiled=True)
    visibilities = pairs(pick, x)
    series = tail(arrived.reshape(-1, spectra), synth_taps, quarters)
    series = series.reshape(2, quarters * spectra, 2, channels).transpose(0, 2, 1, 3)
    return visibilities, series.reshape(2, 1, 2, quarters * spectra * channels)


def solution(mesh):
    in_specs = (P(None, "stn", "beam"), P(), P(), P(None, "stn", "beam", None), P())
    out_specs = (P(None, "stn", "beam", None), P(None, "beam", "stn", None))
    return jax.shard_map(local, mesh=mesh, in_specs=in_specs, out_specs=out_specs, check_vma=False)
```

time: 328 us -> 235 us (0.72)
  waiting for transfers between devices: 164 us -> 79 us
  blocking collectives: 0 us -> 64.9 us
  local copies, waits for them, and re-layouts: 60.3 us -> 15.8 us
  Pallas kernels: 0 us -> 40.4 us
  other arithmetic: 40.4 us -> 1.3 us
  matrix products: 16.5 us -> 1.33 us
  starting transfers between devices: 30.3 us -> 16.8 us
    all_to_all x2 -> x1, waiting for transfers between devices: 83.3 us -> 0.01 us  [local(): lax.all_to_all(formed, 'stn', split_axis=0, concat_axis=0, tiled=True)]
    all_to_all x0 -> x1, blocking collectives: none -> 64.9 us  [local(): lax.all_to_all(spectral, 'stn', split_axis=0, concat_axis=0, tiled=True)]
    pallas_call x0 -> x4, Pallas kernels: none -> 40.4 us  [the longest x1 24.1 us: pairs(): pl.pallas_call(functools.partial(pairs_kernel, 1.0 / (quarters * spectra)...]
    add x1 -> x0, other arithmetic: 22.4 us -> none  [local(): windowed + filter_taps[tap_index][None, :, None, None] * reordered[..., b...]
    dot_general x5 -> x1, matrix products: 16.5 us -> 1.33 us  [local(): lax.dot_general(beam_weights, pick, (((3,), (0,)), ((), ())), preferred_e...]
    all_to_all x2 -> x1, starting transfers between devices: 25.3 us -> 11.9 us  [local(): lax.all_to_all(formed, 'stn', split_axis=0, concat_axis=0, tiled=True)]
    gather x1 -> x0, local copies, waits for them, and re-layouts: 8.23 us -> none  [local(): channel_data = jnp.take(channel_data, inverse, axis=2)]
    reshape x3 -> x2, local copies, waits for them, and re-layouts: 8.12 us -> 0.72 us  [local(): turned.reshape(2, held, owners, 2, stations).transpose(0, 1, 3, 2, 4)]
  transfers between devices with their start and end apart: 4 -> 3, of which waited for: 3 -> 2; matrix products, arithmetic and copies ran while one was open for 6% -> 1% of each run, Pallas kernels for 0% -> 10%
where the time goes in v1:
time: 235 us; the launch traced here: 234 us
  waiting for transfers between devices  79 us (34%)
  blocking collectives  64.9 us (28%)
  Pallas kernels  40.4 us (17%)
  starting transfers between devices  16.8 us (7%)
  local copies, waits for them, and re-layouts  15.8 us (7%)
  between operations  14.2 us (6%)
    all_gather x1, waiting for transfers between devices, local(): x = lax.all_gather(mine, 'beam', axis=0, tiled=False)  77.4 us
    all_to_all x1, blocking collectives, local(): lax.all_to_all(spectral, 'stn', split_axis=0, concat_axis=0, tiled=True)  64.9 us
    pallas_call x1, Pallas kernels, pairs(): pl.pallas_call(functools.partial(pairs_kernel, 1.0 / (quarters * spectra)...  24.1 us
    unnamed x24, local copies, waits for them, and re-layouts  12.5 us
    all_to_all x1, starting transfers between devices, local(): lax.all_to_all(formed, 'stn', split_axis=0, concat_axis=0, tiled=True)  11.9 us
    pallas_call x1, Pallas kernels, front(): pl.pallas_call(functools.partial(front_kernel, taps, channels), out_shape...  7.82 us
    ppermute x1, starting transfers between devices, from_behind(): return lax.ppermute(block, axis, route)  4.92 us
  transfers between devices with their start and end apart: 3, of which 2 were waited for; matrix products, arithmetic and copies ran while one was open for 1% of the time, Pallas kernels for 10%

profile of v1, /device:TPU:1, one launch (start us, length us, event | category | flops | bytes accessed | tf_op | source)
XLA Modules:
  0.0 233.6 jit_solution(12208219526915046382)
XLA Ops:
  7.2 1.0 slice.11
  8.2 4.9 %collective-permute-start = (bf16[2,16,1408]{2,1,0:T(8,128)(2,1)S(1)}, bf16[2,16,1408]{2,1,0:T(8,128)(2,1)S(1)}, u32[]{:S(2)}, u32[]{:S(2)}) collective-permute-start(bf16[2,16,1408]{2,1,0:T(8,128)(2,1)S(1)} %slice.11), channel_id=1, source_target_pairs={{0,1},{1,2},{2,3},{4,5},{5,6},{6,7},{8,9},{9,10},{10,11},{12,13},{... | collective-permute-start | bytes 270344 | tf_op jit(solution)/shard_map/ppermute | solution.py:243
  13.1 1.5 collective-permute-done.h_ref
  14.7 1.6 copy-done.4
  16.3 0.9 copy-done.5
  17.2 0.9 copy-done.6
  18.1 0.7 copy-done.9
  18.8 7.8 %front.1 = bf16[4096,256]{1,0:T(8,128)(2,1)S(1)} custom-call(bf16[2,16,32768]{2,1,0:T(8,128)(2,1)S(1)} %copy-done.4, bf16[2,16,1408]{2,1,0:T(8,128)(2,1)S(1)} %collective-permute-done.h_ref, f32[12,128]{1,0:T(8,128)S(1)} %copy-done.9, bf16[256,256]{1,0:T(8,128)(2,1)S(1)} %copy-done.6, bf16[256,256]{1,0:T(8,128)(2,1)S(1)} %copy-done.5), custom_call_target="tpu_custom_call" | custom-call | tf_op jit(solution)/shard_map/front/pallas_call | solution.py:95
  26.6 64.9 %all_to_all.10 = bf16[64,2,2,16,256]{4,3,2,1,0:T(8,128)(2,1)S(1)} all-to-all(bf16[64,2,2,16,256]{4,3,2,1,0:T(8,128)(2,1)S(1)} %bitcast.40), channel_id=1, replica_groups=mesh['stn'=64,'beam'=4] {'stn'}, dimensions={0} | all-to-all | bytes 4194304 | tf_op jit(solution)/shard_map/all_to_all | solution.py:264
  91.5 1.5 copy.18
  93.1 0.7 copy-done.11
  93.7 1.3 fusion.8
  95.1 0.4 reshape.24
  95.5 0.3 copy.24
  96.1 0.2 pad_maximum_fusion
  96.3 77.4 %all-gather.2.cloned.1.call-done.x_ref = bf16[4,2,2,1024,256]{4,3,2,1,0:T(8,128)(2,1)} async-done(((bf16[1,2,2,1024,256]{4,3,2,1,0:T(8,128)(2,1)}), bf16[4,2,2,1024,256]{4,3,2,1,0:T(8,128)(2,1)}) %all-gather.2.cloned.1.call-update) | async-done | bytes 8388624 | tf_op jit(solution)/shard_map/all_gather | solution.py:266
  173.7 3.4 %copy-done.1 = bf16[4,2,2,1024,256]{4,3,2,1,0:T(8,128)(2,1)S(1)} copy-done((bf16[4,2,2,1024,256]{4,3,2,1,0:T(8,128)(2,1)S(1)}, bf16[4,2,2,1024,256]{4,3,2,1,0:T(8,128)(2,1)}, u32[]{:S(2)}) %copy-start.1) | copy-done | bytes 8388632
  177.1 4.5 %beams.1 = bf16[64,2,16,256]{3,2,1,0:T(8,128)(2,1)S(1)} custom-call(bf16[2,256,2048]{2,1,0:T(8,128)(2,1)S(1)} %bitcast.41, bf16[4,2,2,1024,256]{4,3,2,1,0:T(8,128)(2,1)S(1)} %copy-done.1), custom_call_target="tpu_custom_call" | custom-call | flops 2147483648 | bytes 12582912 | tf_op jit(solution)/shard_map/beams/pallas_call | solution.py:129
  181.6 1.0 copy-done.3
  182.6 11.9 %all-to-all-start.1 = ((bf16[64,2,16,256]{3,2,1,0:T(8,128)(2,1)}), bf16[64,2,16,256]{3,2,1,0:T(8,128)(2,1)S(1)}, u32[]{:S(2)}, u32[]{:S(2)}) async-start(bf16[64,2,16,256]{3,2,1,0:T(8,128)(2,1)} %copy-done.3), calls=%async_computation.1 | async-start | bytes 2097152 | tf_op jit(solution)/shard_map/all_to_all | solution.py:268
  194.5 0.9 fusion.1.pick_ref
  195.4 3.4 %copy-done.2 = bf16[4,2,2,1024,256]{4,3,2,1,0:T(8,128)(2,1)S(1)} copy-done((bf16[4,2,2,1024,256]{4,3,2,1,0:T(8,128)(2,1)S(1)}, bf16[4,2,2,1024,256]{4,3,2,1,0:T(8,128)(2,1)}, u32[]{:S(2)}) %copy-start.2) | copy-done | bytes 8388632
  198.8 24.1 %pairs.1 = f32[2,2,256,1024]{3,2,1,0:T(8,128)} custom-call(bf16[1024,1024]{1,0:T(8,128)(2,1)S(1)} %fusion.1.pick_ref, bf16[4,2,2,1024,256]{4,3,2,1,0:T(8,128)(2,1)S(1)} %copy-done.2), custom_call_target="tpu_custom_call" | custom-call | flops 12884901888 | bytes 16777216 | tf_op jit(solution)/shard_map/pairs/pallas_call | solution.py:173
  222.9 3.9 %tail.1 = f32[2,2048,128]{2,1,0:T(8,128)} custom-call(bf16[2048,256]{1,0:T(8,128)(2,1)S(1)} %bitcast.42, f32[12,128]{1,0:T(8,128)S(1)} %copy-done.10, bf16[256,256]{1,0:T(8,128)(2,1)S(1)} %copy-done.8, bf16[256,256]{1,0:T(8,128)(2,1)S(1)} %copy-done.7), custom_call_target="tpu_custom_call" | custom-call | tf_op jit(solution)/shard_map/tail/pallas_call | solution.py:229
  (22 shorter events, 0.4 us)
Async XLA Ops:
  7.2 85.9 %copy-start = (bf16[2,2,128,1024]{3,2,1,0:T(8,128)(2,1)S(1)}, bf16[2,2,128,1024]{3,2,1,0:T(8,128)(2,1)}, u32[]{:S(2)}) copy-start(bf16[2,2,128,1024]{3,2,1,0:T(8,128)(2,1)} %param.12) | copy-start | bytes 3145732
  7.2 166.5 %all-gather.2.cloned.1.call-start = ((), (), s32[]{:S(2)}) async-start(), calls=%async_computation.2 | async-start | bytes 10485760 | tf_op jit(solution)/shard_map/all_gather | solution.py:266
  8.2 6.5 %collective-permute-start = (bf16[2,16,1408]{2,1,0:T(8,128)(2,1)S(1)}, bf16[2,16,1408]{2,1,0:T(8,128)(2,1)S(1)}, u32[]{:S(2)}, u32[]{:S(2)}) collective-permute-start(bf16[2,16,1408]{2,1,0:T(8,128)(2,1)S(1)} %slice.11), channel_id=1, source_target_pairs={{0,1},{1,2},{2,3},{4,5},{5,6},{6,7},{8,9},{9,10},{10,11},{12,13},{... | collective-permute-start | bytes 270344 | tf_op jit(solution)/shard_map/ppermute | solution.py:243
  14.7 1.6 copy-start.4
  16.3 0.9 copy-start.5
  17.2 0.9 copy-start.6
  18.1 0.7 copy-start.9
  93.0 0.7 copy-start.11
  173.7 3.4 %copy-start.1 = (bf16[4,2,2,1024,256]{4,3,2,1,0:T(8,128)(2,1)S(1)}, bf16[4,2,2,1024,256]{4,3,2,1,0:T(8,128)(2,1)}, u32[]{:S(2)}) copy-start(bf16[4,2,2,1024,256]{4,3,2,1,0:T(8,128)(2,1)} %all-gather.2.cloned.1.call-done.x_ref) | copy-start | bytes 25165828
  181.6 1.0 copy-start.3
  182.6 40.3 %all-to-all-start.1 = ((bf16[64,2,16,256]{3,2,1,0:T(8,128)(2,1)}), bf16[64,2,16,256]{3,2,1,0:T(8,128)(2,1)S(1)}, u32[]{:S(2)}, u32[]{:S(2)}) async-start(bf16[64,2,16,256]{3,2,1,0:T(8,128)(2,1)} %copy-done.3), calls=%async_computation.1 | async-start | bytes 2097152 | tf_op jit(solution)/shard_map/all_to_all | solution.py:268
  195.4 3.4 %copy-start.2 = (bf16[4,2,2,1024,256]{4,3,2,1,0:T(8,128)(2,1)S(1)}, bf16[4,2,2,1024,256]{4,3,2,1,0:T(8,128)(2,1)}, u32[]{:S(2)}) copy-start(bf16[4,2,2,1024,256]{4,3,2,1,0:T(8,128)(2,1)} %all-gather.2.cloned.1.call-done.x_ref) | copy-start | bytes 25165828
  198.7 24.1 %copy-start.7 = (bf16[256,256]{1,0:T(8,128)(2,1)S(1)}, bf16[256,256]{1,0:T(8,128)(2,1)}, u32[]{:S(2)}) copy-start(bf16[256,256]{1,0:T(8,128)(2,1)} %constant.11.clone.low_ref) | copy-start | bytes 393220
  198.7 24.1 %copy-start.8 = (bf16[256,256]{1,0:T(8,128)(2,1)S(1)}, bf16[256,256]{1,0:T(8,128)(2,1)}, u32[]{:S(2)}) copy-start(bf16[256,256]{1,0:T(8,128)(2,1)} %constant.10.clone.high_ref) | copy-start | bytes 393220
  198.8 24.1 %copy-start.10 = (f32[12,128]{1,0:T(8,128)S(1)}, f32[12,128]{1,0:T(8,128)}, u32[]{:S(2)}) copy-start(f32[12,128]{1,0:T(8,128)} %taps_ref.3) | copy-start | bytes 18436
Sparse Core Ops, SparseCore 0:
  93.2 80.4 all-gather.1

commit v2 on v1

--- a/solution.py
+++ b/solution.py
@@ -102,6 +102,125 @@
         compiler_params=pltpu.CompilerParams(vmem_limit_bytes=40 * MIB),
         name="front",
     )(voltages, history, filter_taps, high, low)
+
+MESH = pl.DeviceIdType.MESH
+
+
+def turn_kernel(sides, planes, across, s_ref, x_ref, send, arrive, forward, forwarded, share, shared):
+    pairs_count = lax.axis_size("stn") // planes
+    stn, beam = lax.axis_index("stn"), lax.axis_index("beam")
+    p, place = stn // planes, stn % planes
+    x, y = place // across, place % across
+    side, core = beam // 2, beam % 2
+    rows = s_ref.shape[3]
+    partner, sibling = (stn, (1 - side) * 2 + core), (stn, side * 2 + 1 - core)
+
+    def target(turns, dx, dy):
+        enter = (side, 0, 1 - side, 1)[turns]
+        return ((p + turns) % pairs_count) * planes + ((x + dx) % across) * across + (y + dy) % across, enter * 2 + core
+
+    def origin(group, at):
+        near = (p + 3 + 2 * at) % pairs_count
+        return ((p, at), (near, 0), (near, 1), ((p + 2) % pairs_count, 1 - at))[group]
+
+    def part(group, at, dx):
+        pair, start = origin(group, at)
+        first = pl.multiple_of((pair * planes + ((x + across - dx) % across) * across) * rows, across * rows)
+        return x_ref.at[start * 2 + core, :, :, pl.ds(first, across * rows), :], start
+
+    def copy(source, goal, out, into, device):
+        return pltpu.make_async_remote_copy(
+            src_ref=source, dst_ref=goal, send_sem=out, recv_sem=into, device_id=device, device_id_type=MESH
+        )
+
+    barrier = pltpu.get_barrier_semaphore()
+    for other in (partner, sibling):
+        pl.semaphore_signal(barrier, inc=1, device_id=other, device_id_type=MESH)
+
+    @pl.loop(0, planes)
+    def _(i):
+        for group in range(4):
+            pair, start = origin(group, side)
+            other = (pair * planes + i, start * 2 + core)
+
+            def greet(other=other):
+                pl.semaphore_signal(barrier, inc=1, device_id=other, device_id_type=MESH)
+
+            if group:
+                greet()
+            else:
+                pl.when(i != place)(greet)
+
+    pl.semaphore_wait(barrier, 4 * planes - 1 + 2)
+
+    first = pl.multiple_of(stn * rows, rows)
+    landing = x_ref.at[beam, :, :, pl.ds(first, rows), :]
+
+    @pl.loop(0, planes)
+    def _(i):
+        dx, dy = i // across, i % across
+        for turns, slot in ((2, 3), (1, 1 + side), (3, 1 + side), (0, 0)):
+            owner, entry = target(turns, dx, dy)
+
+            def go(owner=owner, entry=entry, slot=slot):
+                copy(s_ref.at[owner], landing, send, arrive.at[slot, dx], (owner, entry)).start()
+
+            if turns:
+                go()
+            else:
+                pl.when(i != 0)(go)
+
+                @pl.when(i == 0)
+                def _():
+                    pltpu.make_async_copy(s_ref.at[stn], landing, arrive.at[0, 0]).start()
+
+    def wait(ref, sem):
+        pltpu.make_async_copy(ref, ref, sem).wait()
+
+    def entered(dx):
+        for group in (3, 1, 2, 0):
+            block, start = part(group, side, dx)
+            wait(block, arrive.at[group, dx])
+            copy(block, block, forward, forwarded.at[group, dx], partner).start()
+            copy(block, block, share.at[start], shared.at[start], sibling).start()
+
+    def passed(dx):
+        for group in (3, 1, 2, 0):
+            block, start = part(group, 1 - side, dx)
+            wait(block, forwarded.at[group, dx])
+            copy(block, block, share.at[start], shared.at[start], sibling).start()
+
+    @pl.loop(0, across + 1)
+    def _(step):
+        @pl.when(step < across)
+        def _():
+            entered(step)
+
+        @pl.when(step > 0)
+        def _():
+            passed(step - 1)
+
+    for start in range(sides):
+        wait(x_ref.at[start * 2 + 1 - core], shared.at[start])
+        wait(x_ref.at[start * 2 + core], share.at[start])
+    wait(x_ref.at[0], forward)
+    wait(s_ref.at[pl.ds(0, 4 * planes - 1)], send)
+
+
+def turn(spectral):
+    owners, channels, parts, rows, spectra = spectral.shape
+    quarters = lax.axis_size("beam")
+    across = 4
+    dma = pltpu.SemaphoreType.DMA
+    return pl.pallas_call(
+        functools.partial(turn_kernel, quarters // 2, across * across, across),
+        out_shape=jax.ShapeDtypeStruct((quarters, channels, parts, owners * rows, spectra), BF16),
+        in_specs=[pl.BlockSpec(memory_space=pl.ANY)],
+        out_specs=pl.BlockSpec(memory_space=pl.ANY),
+        scratch_shapes=[dma, dma((4, across)), dma, dma((4, across)), dma((2,)), dma((2,))],
+        compiler_params=pltpu.CompilerParams(collective_id=0, has_side_effects=True),
+        name="turn",
+    )(spectral)
 
 
 def beams_kernel(quarters, w_ref, x_ref, out_ref, left_ref, right_ref):
@@ -261,9 +380,7 @@
     weights = jnp.stack([real_rows, imag_rows], axis=2).reshape(held, 4 * owners, 2 * stations)
 
     spectral = front(voltages, history, filter_taps).reshape(owners, held, 2, rows, spectra)
-    mine = lax.all_to_all(spectral, "stn", split_axis=0, concat_axis=0, tiled=True)
-    mine = mine.transpose(1, 2, 0, 3, 4).reshape(held, 2, stations, spectra)
-    x = lax.all_gather(mine, "beam", axis=0, tiled=False)
+    x = turn(spectral)
     formed = beams(weights, x)
     arrived = lax.all_to_all(formed, "stn", split_axis=0, concat_axis=0, tiled=True)
     visibilities = pairs(pick, x)

time: 235 us -> 159 us (0.68)
  Pallas kernels: 40.4 us -> 129 us
  waiting for transfers between devices: 79 us -> 0.01 us
  blocking collectives: 64.9 us -> 0 us
  between operations: 14.2 us -> 0.84 us
  starting transfers between devices: 16.8 us -> 11.5 us
  local copies, waits for them, and re-layouts: 15.8 us -> 12.2 us
    pallas_call x0 -> x1, Pallas kernels: none -> 88.7 us  [turn(): pl.pallas_call(functools.partial(turn_kernel, quarters // 2, across * acr...]
    all_gather x1 -> x0, waiting for transfers between devices: 77.4 us -> none  [local(): x = lax.all_gather(mine, 'beam', axis=0, tiled=False)]
    all_to_all x1 -> x0, blocking collectives: 64.9 us -> none  [local(): lax.all_to_all(spectral, 'stn', split_axis=0, concat_axis=0, tiled=True)]
    all_to_all x1, starting transfers between devices: 11.9 us -> 6.57 us  [local(): lax.all_to_all(formed, 'stn', split_axis=0, concat_axis=0, tiled=True)]
    unnamed x24 -> x26, local copies, waits for them, and re-layouts: 12.5 us -> 10.4 us
  transfers between devices with their start and end apart: 3 -> 2, of which waited for: 2 -> 0; matrix products, arithmetic and copies ran while one was open for 1% -> 3% of each run, Pallas kernels for 10% -> 15%
where the time goes in v2:
time: 159 us; the launch traced here: 157 us
  Pallas kernels  129 us (81%)
  local copies, waits for them, and re-layouts  12.2 us (8%)
  starting transfers between devices  11.5 us (7%)
  matrix products  2.02 us (1%)
    pallas_call x1, Pallas kernels, turn(): pl.pallas_call(functools.partial(turn_kernel, quarters // 2, across * acr...  88.7 us
    pallas_call x1, Pallas kernels, pairs(): pl.pallas_call(functools.partial(pairs_kernel, 1.0 / (quarters * spectra)...  24.1 us
    unnamed x26, local copies, waits for them, and re-layouts  10.4 us
    pallas_call x1, Pallas kernels, front(): pl.pallas_call(functools.partial(front_kernel, taps, channels), out_shape...  7.82 us
    all_to_all x1, starting transfers between devices, local(): lax.all_to_all(formed, 'stn', split_axis=0, concat_axis=0, tiled=True)  6.57 us
    ppermute x1, starting transfers between devices, from_behind(): return lax.ppermute(block, axis, route)  4.92 us
    pallas_call x1, Pallas kernels, beams(): pl.pallas_call(functools.partial(beams_kernel, quarters), grid=(channels,...  4.52 us
    pallas_call x1, Pallas kernels, tail(): pl.pallas_call(functools.partial(tail_kernel, taps, quarters), out_shape=...  3.92 us
  transfers between devices with their start and end apart: 2, of which 0 were waited for; matrix products, arithmetic and copies ran while one was open for 3% of the time, Pallas kernels for 15%

profile of v2, /device:TPU:1, one launch (start us, length us, event | category | flops | bytes accessed | tf_op | source)
XLA Modules:
  0.0 156.9 jit_solution(7527997974767249745)
XLA Ops:
  0.6 0.0 copy-start
  0.6 1.0 slice.11
  1.6 4.9 %collective-permute-start = (bf16[2,16,1408]{2,1,0:T(8,128)(2,1)S(1)}, bf16[2,16,1408]{2,1,0:T(8,128)(2,1)S(1)}, u32[]{:S(2)}, u32[]{:S(2)}) collective-permute-start(bf16[2,16,1408]{2,1,0:T(8,128)(2,1)S(1)} %slice.11), channel_id=1, source_target_pairs={{0,1},{1,2},{2,3},{4,5},{5,6},{6,7},{8,9},{9,10},{10,11},{12,13},{... | collective-permute-start | bytes 270344 | tf_op jit(solution)/shard_map/ppermute | solution.py:362
  6.6 2.0 %fusion.8 = bf16[2,2,128,1024]{3,2,1,0:T(8,128)(2,1)S(1)} fusion(bf16[2,2,128,1024]{3,2,1,0:T(8,128)(2,1)S(1)} %copy-done, s32[1024]{0:T(1024)} %param.13), kind=kOutput, calls=%fused_computation.7 | convolution fusion | flops 1075314688 | bytes 2101248 | tf_op jit(solution)/shard_map/dot_general | solution.py:376
  8.6 0.4 reshape.24
  9.0 0.3 copy.16
  9.4 0.1 slice_bitcast_fusion
  9.5 0.2 maximum_bitcast_fusion
  9.7 0.0 copy-start.6
  9.7 0.0 copy-start.7
  9.7 0.0 copy-start.10
  9.7 0.2 pad_maximum_fusion
  9.9 1.3 copy-done.5
  11.3 7.8 %front.1 = bf16[4096,256]{1,0:T(8,128)(2,1)S(1)} custom-call(bf16[2,16,32768]{2,1,0:T(8,128)(2,1)S(1)} %copy-done.5, bf16[2,16,1408]{2,1,0:T(8,128)(2,1)S(1)} %collective-permute-done.h_ref, f32[12,128]{1,0:T(8,128)S(1)} %copy-done.10, bf16[256,256]{1,0:T(8,128)(2,1)S(1)} %copy-done.7, bf16[256,256]{1,0:T(8,128)(2,1)S(1)} %copy-done.6), custom_call_target="tpu_custom_call" | custom-call | tf_op jit(solution)/shard_map/front/pallas_call | solution.py:95
  19.1 1.3 copy-done.3
  20.4 88.7 %turn.1.x_ref = bf16[4,2,2,1024,256]{4,3,2,1,0:T(8,128)(2,1)} custom-call(bf16[64,2,2,16,256]{4,3,2,1,0:T(8,128)(2,1)} %bitcast.37), custom_call_target="tpu_custom_call" | custom-call | tf_op jit(solution)/shard_map/turn/pallas_call | solution.py:215
  109.2 3.4 %copy-done.1 = bf16[4,2,2,1024,256]{4,3,2,1,0:T(8,128)(2,1)S(1)} copy-done((bf16[4,2,2,1024,256]{4,3,2,1,0:T(8,128)(2,1)S(1)}, bf16[4,2,2,1024,256]{4,3,2,1,0:T(8,128)(2,1)}, u32[]{:S(2)}) %copy-start.1) | copy-done | bytes 8388632
  112.5 4.5 %beams.1 = bf16[64,2,16,256]{3,2,1,0:T(8,128)(2,1)S(1)} custom-call(bf16[2,256,2048]{2,1,0:T(8,128)(2,1)S(1)} %bitcast.38, bf16[4,2,2,1024,256]{4,3,2,1,0:T(8,128)(2,1)S(1)} %copy-done.1), custom_call_target="tpu_custom_call" | custom-call | flops 2147483648 | bytes 12582912 | tf_op jit(solution)/shard_map/beams/pallas_call | solution.py:248
  117.1 1.0 copy-done.4
  118.0 6.6 %all-to-all-start = ((bf16[64,2,16,256]{3,2,1,0:T(8,128)(2,1)}), bf16[64,2,16,256]{3,2,1,0:T(8,128)(2,1)S(1)}, u32[]{:S(2)}, u32[]{:S(2)}) async-start(bf16[64,2,16,256]{3,2,1,0:T(8,128)(2,1)} %copy-done.4), calls=%async_computation | async-start | bytes 2097152 | tf_op jit(solution)/shard_map/all_to_all | solution.py:385
  124.6 0.9 fusion.1.pick_ref
  125.5 3.4 %copy-done.2 = bf16[4,2,2,1024,256]{4,3,2,1,0:T(8,128)(2,1)S(1)} copy-done((bf16[4,2,2,1024,256]{4,3,2,1,0:T(8,128)(2,1)S(1)}, bf16[4,2,2,1024,256]{4,3,2,1,0:T(8,128)(2,1)}, u32[]{:S(2)}) %copy-start.2) | copy-done | bytes 8388632
  128.9 24.1 %pairs.1 = f32[2,2,256,1024]{3,2,1,0:T(8,128)} custom-call(bf16[1024,1024]{1,0:T(8,128)(2,1)S(1)} %fusion.1.pick_ref, bf16[4,2,2,1024,256]{4,3,2,1,0:T(8,128)(2,1)S(1)} %copy-done.2), custom_call_target="tpu_custom_call" | custom-call | flops 12884901888 | bytes 16777216 | tf_op jit(solution)/shard_map/pairs/pallas_call | solution.py:292
  153.0 3.9 %tail.1 = f32[2,2048,128]{2,1,0:T(8,128)} custom-call(bf16[2048,256]{1,0:T(8,128)(2,1)S(1)} %bitcast.39, f32[12,128]{1,0:T(8,128)S(1)} %copy-done.11, bf16[256,256]{1,0:T(8,128)(2,1)S(1)} %copy-done.9, bf16[256,256]{1,0:T(8,128)(2,1)S(1)} %copy-done.8), custom_call_target="tpu_custom_call" | custom-call | tf_op jit(solution)/shard_map/tail/pallas_call | solution.py:348
  (20 shorter events, 0.1 us)
Async XLA Ops:
  0.6 5.9 %copy-start = (bf16[2,2,128,1024]{3,2,1,0:T(8,128)(2,1)S(1)}, bf16[2,2,128,1024]{3,2,1,0:T(8,128)(2,1)}, u32[]{:S(2)}) copy-start(bf16[2,2,128,1024]{3,2,1,0:T(8,128)(2,1)} %param.12) | copy-start | bytes 3145732
  1.6 8.3 %collective-permute-start = (bf16[2,16,1408]{2,1,0:T(8,128)(2,1)S(1)}, bf16[2,16,1408]{2,1,0:T(8,128)(2,1)S(1)}, u32[]{:S(2)}, u32[]{:S(2)}) collective-permute-start(bf16[2,16,1408]{2,1,0:T(8,128)(2,1)S(1)} %slice.11), channel_id=1, source_target_pairs={{0,1},{1,2},{2,3},{4,5},{5,6},{6,7},{8,9},{9,10},{10,11},{12,13},{... | collective-permute-start | bytes 270344 | tf_op jit(solution)/shard_map/ppermute | solution.py:362
  9.7 1.6 %copy-start.5 = (bf16[2,16,32768]{2,1,0:T(8,128)(2,1)S(1)}, bf16[2,16,32768]{2,1,0:T(8,128)(2,1)}, u32[]{:S(2)}) copy-start(bf16[2,16,32768]{2,1,0:T(8,128)(2,1)} %v_ref.1) | copy-start | bytes 6291460
  9.7 1.6 %copy-start.6 = (bf16[256,256]{1,0:T(8,128)(2,1)S(1)}, bf16[256,256]{1,0:T(8,128)(2,1)}, u32[]{:S(2)}) copy-start(bf16[256,256]{1,0:T(8,128)(2,1)} %constant.9.clone.low_ref) | copy-start | bytes 393220
  9.7 1.6 %copy-start.7 = (bf16[256,256]{1,0:T(8,128)(2,1)S(1)}, bf16[256,256]{1,0:T(8,128)(2,1)}, u32[]{:S(2)}) copy-start(bf16[256,256]{1,0:T(8,128)(2,1)} %constant.8.clone.high_ref) | copy-start | bytes 393220
  9.7 1.6 copy-start.10
  19.1 1.3 copy-start.3
  109.2 3.4 %copy-start.1 = (bf16[4,2,2,1024,256]{4,3,2,1,0:T(8,128)(2,1)S(1)}, bf16[4,2,2,1024,256]{4,3,2,1,0:T(8,128)(2,1)}, u32[]{:S(2)}) copy-start(bf16[4,2,2,1024,256]{4,3,2,1,0:T(8,128)(2,1)} %turn.1.x_ref) | copy-start | bytes 25165828
  117.1 1.0 copy-start.4
  118.0 6.6 %copy-start.12 = (s32[1024]{0:T(1024)S(1)}, s32[1024]{0:T(1024)}, u32[]{:S(2)}) copy-start(s32[1024]{0:T(1024)} %param.13) | copy-start | bytes 12292
  118.0 35.0 %all-to-all-start = ((bf16[64,2,16,256]{3,2,1,0:T(8,128)(2,1)}), bf16[64,2,16,256]{3,2,1,0:T(8,128)(2,1)S(1)}, u32[]{:S(2)}, u32[]{:S(2)}) async-start(bf16[64,2,16,256]{3,2,1,0:T(8,128)(2,1)} %copy-done.4), calls=%async_computation | async-start | bytes 2097152 | tf_op jit(solution)/shard_map/all_to_all | solution.py:385
  125.5 3.4 %copy-start.2 = (bf16[4,2,2,1024,256]{4,3,2,1,0:T(8,128)(2,1)S(1)}, bf16[4,2,2,1024,256]{4,3,2,1,0:T(8,128)(2,1)}, u32[]{:S(2)}) copy-start(bf16[4,2,2,1024,256]{4,3,2,1,0:T(8,128)(2,1)} %turn.1.x_ref) | copy-start | bytes 25165828
  128.9 24.1 %copy-start.8 = (bf16[256,256]{1,0:T(8,128)(2,1)S(1)}, bf16[256,256]{1,0:T(8,128)(2,1)}, u32[]{:S(2)}) copy-start(bf16[256,256]{1,0:T(8,128)(2,1)} %constant.11.clone.low_ref) | copy-start | bytes 393220
  128.9 24.1 %copy-start.9 = (bf16[256,256]{1,0:T(8,128)(2,1)S(1)}, bf16[256,256]{1,0:T(8,128)(2,1)}, u32[]{:S(2)}) copy-start(bf16[256,256]{1,0:T(8,128)(2,1)} %constant.10.clone.high_ref) | copy-start | bytes 393220
  128.9 24.1 %copy-start.11 = (f32[12,128]{1,0:T(8,128)S(1)}, f32[12,128]{1,0:T(8,128)}, u32[]{:S(2)}) copy-start(f32[12,128]{1,0:T(8,128)} %taps_ref.3) | copy-start | bytes 18436

commit v3 on v1

--- a/solution.py
+++ b/solution.py
@@ -103,87 +103,248 @@
         name="front",
     )(voltages, history, filter_taps, high, low)
 
-
-def beams_kernel(quarters, w_ref, x_ref, out_ref, left_ref, right_ref):
-    q = pl.program_id(1)
-    groups = w_ref.shape[1] // 4
-    stations = x_ref.shape[3]
-    result = dot(w_ref[0, :, :stations], x_ref[0, 0, 0], ((1,), (0,)))
-    result += dot(w_ref[0, :, stations:], x_ref[0, 0, 1], ((1,), (0,)))
-    for i in range(4):
-        rows = result[i * groups : (i + 1) * groups]
-        left_ref[pl.ds(q * 4 + i, groups, stride=16), :] = rows[:, :128]
-        right_ref[pl.ds(q * 4 + i, groups, stride=16), :] = rows[:, 128:]
-
-    @pl.when(q == quarters - 1)
-    def _():
-        for d in range(0, groups, 8):
+MESH = pl.DeviceIdType.MESH
+
+
+def remote(source, goal, out, into, device):
+    return pltpu.make_async_remote_copy(
+        src_ref=source, dst_ref=goal, send_sem=out, recv_sem=into, device_id=device, device_id_type=MESH
+    )
+
+
+def wait(ref, sem):
+    pltpu.make_async_copy(ref, ref, sem).wait()
+
+
+def hail(device):
+    pl.semaphore_signal(pltpu.get_barrier_semaphore(), inc=1, device_id=device, device_id_type=MESH)
+
+
+def turn_kernel(
+    sides, planes, across, s_ref, w_ref, order_ref, x_ref, weights_ref, pick_ref,
+    relay_ref, send, arrive, relayed, onward, forward, forwarded, share, shared,
+):
+    pairs_count = lax.axis_size("stn") // planes
+    stn, beam = lax.axis_index("stn"), lax.axis_index("beam")
+    p, place = stn // planes, stn % planes
+    x, y = place // across, place % across
+    side, core = beam // 2, beam % 2
+    rows = s_ref.shape[3]
+    mine, others = side * 2 + core, (1 - side) * 2 + core
+    partner, sibling = (stn, others), (stn, side * 2 + 1 - core)
+    near = (p + 3 + 2 * side) % pairs_count
+    far = (p + 2) % pairs_count
+    beyond = (p + 1 + 2 * side) % pairs_count
+
+    def part(ref, pair, dx):
+        first = pl.multiple_of((pair * planes + ((x + across - dx) % across) * across) * rows, across * rows)
+        return ref.at[:, :, pl.ds(first, across * rows), :]
+
+    def entering(at, dx):
+        border = (p + 3 + 2 * at) % pairs_count
+        for group, pair, start in ((1, border, at), (3, far, 1 - at), (2, border, 1 - at), (0, p, at)):
+            yield group, part(x_ref.at[start * 2 + core], pair, dx), start
+
+    hail(sibling)
+
+    @pl.loop(0, planes)
+    def _(i):
+        for pair, to in ((p, others), (near, others), (far, others)):
+            hail((pair * planes + i, to))
+
+        @pl.when(i != place)
+        def _():
+            hail((p * planes + i, mine))
+
+    pl.semaphore_wait(pltpu.get_barrier_semaphore(), 4 * planes)
+
+    first = pl.multiple_of(stn * rows, rows)
+    landing = x_ref.at[mine, :, :, pl.ds(first, rows), :]
+
+    @pl.loop(0, planes)
+    def _(i):
+        dx, dy = i // across, i % across
+        goal = ((x + dx) % across) * across + (y + dy) % across
+        remote(s_ref.at[beyond * planes + goal], relay_ref.at[place], send, relayed.at[dx], (p * planes + goal, others)).start()
+        remote(s_ref.at[far * planes + goal], landing, send, arrive.at[3, dx], (far * planes + goal, others)).start()
+        remote(s_ref.at[near * planes + goal], landing, send, arrive.at[2, dx], (near * planes + goal, others)).start()
+
+        @pl.when(i != 0)
+        def _():
+            remote(s_ref.at[p * planes + goal], landing, send, arrive.at[0, dx], (p * planes + goal, mine)).start()
+
+        @pl.when(i == 0)
+        def _():
+            pltpu.make_async_copy(s_ref.at[stn], landing, arrive.at[0, 0]).start()
+
+    stations = order_ref.shape[1]
+
+    @pl.loop(0, stations // 64)
+    def _(i):
+        first = pl.multiple_of(i * 64, 64)
+        station = lax.broadcasted_iota(jnp.int32, (64, stations), 0) + first
+        pick_ref[pl.ds(first, 64), :] = jnp.where(order_ref[...] == station, 1.0, 0.0).astype(BF16)
+
+    def relay(dx):
+        block = relay_ref.at[pl.ds(((x + across - dx) % across) * across, across)]
+        wait(block, relayed.at[dx])
+        for i in range(across):
+            source = (x + across - dx) % across * across + i
+            first = pl.multiple_of((p * planes + source) * rows, rows)
+            goal = x_ref.at[others, :, :, pl.ds(first, rows), :]
+            remote(relay_ref.at[source], goal, onward, arrive.at[1, dx], (near * planes + place, others)).start()
+
+    def entered(dx):
+        for group, block, start in entering(side, dx):
+            wait(block, arrive.at[group, dx])
+            remote(block, block, forward, forwarded.at[group, dx], partner).start()
+            remote(block, block, share.at[start], shared.at[start], sibling).start()
+
+    def passed(dx):
+        for group, block, start in entering(1 - side, dx):
+            wait(block, forwarded.at[group, dx])
+            remote(block, block, share.at[start], shared.at[start], sibling).start()
+
+    @pl.loop(0, across + 2)
+    def _(step):
+        @pl.when(step < across)
+        def _():
+            relay(step)
+
+        @pl.when((step > 0) & (step <= across))
+        def _():
+            entered(step - 1)
+
+        @pl.when(step > 1)
+        def _():
+            passed(step - 2)
+
+        @pl.when(step < w_ref.shape[1])
+        def _():
+            both = jnp.concatenate([w_ref[0, step], w_ref[1, step]], axis=0)
+            half = w_ref.shape[2]
+            for at in range(0, stations, 256):
+                turned = dot(both, pick_ref[:, at : at + 256], ((1,), (0,)))
+                weights_ref[step, :, at : at + 256] = turned.astype(BF16)
+                crossed = jnp.concatenate([-turned[half:], turned[:half]], axis=0)
+                weights_ref[step, :, stations + at : stations + at + 256] = crossed.astype(BF16)
+
+    for start in range(sides):
+        wait(x_ref.at[start * 2 + 1 - core], shared.at[start])
+        wait(x_ref.at[start * 2 + core], share.at[start])
+    wait(x_ref.at[0], forward)
+    wait(relay_ref, onward)
+    wait(s_ref.at[pl.ds(0, 4 * planes - 1)], send)
+
+
+def turn(spectral, beam_weights, station_order):
+    owners, channels, parts, rows, spectra = spectral.shape
+    quarters = lax.axis_size("beam")
+    across = 4
+    planes = across * across
+    stations, group = owners * rows, beam_weights.shape[2]
+    dma = pltpu.SemaphoreType.DMA
+    vmem = pl.BlockSpec(memory_space=pltpu.VMEM)
+    return pl.pallas_call(
+        functools.partial(turn_kernel, quarters // 2, planes, across),
+        out_shape=(
+            jax.ShapeDtypeStruct((quarters, channels, parts, stations, spectra), BF16),
+            jax.ShapeDtypeStruct((channels, 2 * group, 2 * stations), BF16),
+            jax.ShapeDtypeStruct((stations, stations), BF16),
+        ),
+        in_specs=[vmem] * 3,
+        out_specs=(vmem,) * 3,
+        scratch_shapes=[
+            pltpu.VMEM((planes, channels, parts, rows, spectra), BF16),
+            dma, dma((4, across)), dma((across,)), dma, dma, dma((4, across)), dma((2,)), dma((2,)),
+        ],
+        compiler_params=pltpu.CompilerParams(collective_id=0, has_side_effects=True, vmem_limit_bytes=28 * MIB),
+        name="turn",
+    )(spectral, beam_weights, station_order.reshape(1, stations))
+
+
+def middle_kernel(weights_ref, x_ref, pick_ref, vis_ref, got_ref, formed_ref, turned_ref, left_ref, right_ref, send, arrive):
+    stn, beam = lax.axis_index("stn"), lax.axis_index("beam")
+    owners = lax.axis_size("stn")
+    quarters, channels, _, stations, spectra = x_ref.shape
+    group = weights_ref.shape[1] // 2
+
+    @pl.loop(1, owners)
+    def _(i):
+        hail(((stn + i) % owners, beam))
+
+    nn, nt = ((1,), (0,)), ((1,), (1,))
+
+    @pl.loop(0, channels)
+    def _(c):
+        @pl.loop(0, quarters)
+        def _(q):
+            result = dot(weights_ref[c, :, :stations], x_ref[q, c, 0], nn)
+            result += dot(weights_ref[c, :, stations:], x_ref[q, c, 1], nn)
+            for part in range(2):
+                rows = result[part * group : (part + 1) * group]
+                left_ref[pl.ds(q * 2 + part, group, stride=8), :] = rows[:, :128]
+                right_ref[pl.ds(q * 2 + part, group, stride=8), :] = rows[:, 128:]
+
+        for d in range(0, owners, 8):
             at = slice(d * 16, (d + 8) * 16)
-            out_ref[d : d + 8, 0, :, :128] = left_ref[at, :].astype(BF16).reshape(8, 16, 128)
-            out_ref[d : d + 8, 0, :, 128:] = right_ref[at, :].astype(BF16).reshape(8, 16, 128)
-
-
-def beams(weights, x):
+            formed_ref[d : d + 8, c, :, :128] = left_ref[at, :].astype(BF16).reshape(8, 16, 128)
+            formed_ref[d : d + 8, c, :, 128:] = right_ref[at, :].astype(BF16).reshape(8, 16, 128)
+
+    pl.semaphore_wait(pltpu.get_barrier_semaphore(), owners - 1)
+    pltpu.make_async_copy(formed_ref.at[stn], got_ref.at[stn], arrive).start()
+
+    @pl.loop(1, owners)
+    def _(i):
+        owner = (stn + i) % owners
+        remote(formed_ref.at[owner], got_ref.at[stn], send, arrive, (owner, beam)).start()
+
+    count = vis_ref.shape[2]
+    start = pl.multiple_of(beam * count, count)
+    scale = 1.0 / (quarters * spectra)
+
+    @pl.loop(0, channels)
+    def _(c):
+        for q in range(quarters):
+            at = slice(q * spectra, (q + 1) * spectra)
+            for part in range(2):
+                for r in range(0, stations, 256):
+                    turned_ref[part, r : r + 256, at] = dot(pick_ref[r : r + 256, :], x_ref[q, c, part], nn).astype(BF16)
+        real_rows = turned_ref[0, pl.ds(start, count), :]
+        imag_rows = turned_ref[1, pl.ds(start, count), :]
+        for at in range(0, stations, 256):
+            cols = slice(at, at + 256)
+            real, imag = turned_ref[0, cols, :], turned_ref[1, cols, :]
+            vis_ref[0, c, :, cols] = (dot(real_rows, real, nt) + dot(imag_rows, imag, nt)) * scale
+            vis_ref[1, c, :, cols] = (dot(imag_rows, real, nt) - dot(real_rows, imag, nt)) * scale
+
+    wait(got_ref, arrive)
+    wait(formed_ref.at[pl.ds(0, owners - 1)], send)
+
+
+def middle(weights, x, pick):
     quarters, channels, _, stations, spectra = x.shape
-    groups = weights.shape[1] // 4
+    owners = lax.axis_size("stn")
+    dma = pltpu.SemaphoreType.DMA
+    vmem = pl.BlockSpec(memory_space=pltpu.VMEM)
     return pl.pallas_call(
-        functools.partial(beams_kernel, quarters),
-        grid=(channels, quarters),
-        out_shape=jax.ShapeDtypeStruct((groups, channels, 16, spectra), BF16),
-        in_specs=[
-            pl.BlockSpec((1, 4 * groups, 2 * stations), lambda c, q: (c, 0, 0)),
-            pl.BlockSpec((1, 1, 2, stations, spectra), lambda c, q: (q, c, 0, 0, 0)),
+        middle_kernel,
+        out_shape=(
+            jax.ShapeDtypeStruct((2, channels, stations // quarters, stations), F32),
+            jax.ShapeDtypeStruct((owners, channels, 16, spectra), BF16),
+        ),
+        in_specs=[vmem] * 3,
+        out_specs=(vmem,) * 2,
+        scratch_shapes=[
+            pltpu.VMEM((owners, channels, 16, spectra), BF16),
+            pltpu.VMEM((2, stations, quarters * spectra), BF16),
+            pltpu.VMEM((owners * 16, 128), F32),
+            pltpu.VMEM((owners * 16, 128), F32),
+            dma, dma,
         ],
-        out_specs=pl.BlockSpec((groups, 1, 16, spectra), lambda c, q: (0, c, 0, 0)),
-        scratch_shapes=[pltpu.VMEM((groups * 16, 128), F32)] * 2,
-        compiler_params=pltpu.CompilerParams(vmem_limit_bytes=40 * MIB),
-        cost_estimate=pl.CostEstimate(flops=2 * 2**30, bytes_accessed=12 * MIB, transcendentals=0),
-        name="beams",
-    )(weights, x)
-
-
-def pairs_kernel(scale, pick_ref, x_ref, out_ref, turned_ref, rows_ref):
-    q = pl.program_id(1)
-    stations = x_ref.shape[3]
-    count = out_ref.shape[2]
-    start = pl.multiple_of(lax.axis_index("beam") * count, count)
-    for part in range(2):
-        for r in range(0, stations, 256):
-            turned_ref[part, r : r + 256, :] = dot(pick_ref[r : r + 256, :], x_ref[0, 0, part], ((1,), (0,))).astype(BF16)
-        rows_ref[part] = turned_ref[part, pl.ds(start, count), :]
-    nt = ((1,), (1,))
-    for at in range(0, stations, 256):
-        cols = slice(at, at + 256)
-        real = dot(rows_ref[0], turned_ref[0, cols], nt) + dot(rows_ref[1], turned_ref[1, cols], nt)
-        imag = dot(rows_ref[1], turned_ref[0, cols], nt) - dot(rows_ref[0], turned_ref[1, cols], nt)
-
-        @pl.when(q == 0)
-        def _():
-            out_ref[0, 0, :, cols] = real * scale
-            out_ref[1, 0, :, cols] = imag * scale
-
-        @pl.when(q > 0)
-        def _():
-            out_ref[0, 0, :, cols] += real * scale
-            out_ref[1, 0, :, cols] += imag * scale
-
-
-def pairs(pick, x):
-    quarters, channels, _, stations, spectra = x.shape
-    return pl.pallas_call(
-        functools.partial(pairs_kernel, 1.0 / (quarters * spectra)),
-        grid=(channels, quarters),
-        out_shape=jax.ShapeDtypeStruct((2, channels, stations // quarters, stations), F32),
-        in_specs=[
-            pl.BlockSpec((stations, stations), lambda c, q: (0, 0)),
-            pl.BlockSpec((1, 1, 2, stations, spectra), lambda c, q: (q, c, 0, 0, 0)),
-        ],
-        out_specs=pl.BlockSpec((2, 1, stations // quarters, stations), lambda c, q: (0, c, 0, 0)),
-        scratch_shapes=[pltpu.VMEM((2, stations, spectra), BF16), pltpu.VMEM((2, stations // quarters, spectra), BF16)],
-        compiler_params=pltpu.CompilerParams(vmem_limit_bytes=40 * MIB),
-        cost_estimate=pl.CostEstimate(flops=12 * 2**30, bytes_accessed=16 * MIB, transcendentals=0),
-        name="pairs",
-    )(pick, x)
+        compiler_params=pltpu.CompilerParams(collective_id=1, has_side_effects=True, vmem_limit_bytes=28 * MIB),
+        name="middle",
+    )(weights, x, pick)
 
 
 def tail_kernel(taps, quarters, g_ref, taps_ref, high_ref, low_ref, out_ref, left_ref, right_ref, *lines):
@@ -199,7 +360,7 @@
         for q in range(quarters):
             parts = [
                 jnp.concatenate(
-                    [ref[pl.ds(q * 4 + j * 2 + ri, channels, stride=16), :] for ref in (left_ref, right_ref)], axis=1
+                    [ref[pl.ds(j * 8 + q * 2 + ri, channels, stride=16), :] for ref in (left_ref, right_ref)], axis=1
                 )
                 for ri in range(2)
             ]
@@ -253,20 +414,9 @@
     held = channels // owners
     history = from_behind(voltages[:, :, voltages.shape[2] - (taps - 1) * channels :], "beam", 1)
 
-    pick = (station_order[None, :] == jnp.arange(stations, dtype=jnp.int32)[:, None]).astype(BF16)
-    turned = lax.dot_general(beam_weights, pick, (((3,), (0,)), ((), ())), preferred_element_type=F32).astype(BF16)
-    turned = turned.reshape(2, held, owners, 2, stations).transpose(0, 1, 3, 2, 4)
-    real_rows = jnp.concatenate([turned[0], -turned[1]], axis=-1)
-    imag_rows = jnp.concatenate([turned[1], turned[0]], axis=-1)
-    weights = jnp.stack([real_rows, imag_rows], axis=2).reshape(held, 4 * owners, 2 * stations)
-
     spectral = front(voltages, history, filter_taps).reshape(owners, held, 2, rows, spectra)
-    mine = lax.all_to_all(spectral, "stn", split_axis=0, concat_axis=0, tiled=True)
-    mine = mine.transpose(1, 2, 0, 3, 4).reshape(held, 2, stations, spectra)
-    x = lax.all_gather(mine, "beam", axis=0, tiled=False)
-    formed = beams(weights, x)
-    arrived = lax.all_to_all(formed, "stn", split_axis=0, concat_axis=0, tiled=True)
-    visibilities = pairs(pick, x)
+    x, weights, pick = turn(spectral, beam_weights, station_order)
+    visibilities, arrived = middle(weights, x, pick)
     series = tail(arrived.reshape(-1, spectra), synth_taps, quarters)
     series = series.reshape(2, quarters * spectra, 2, channels).transpose(0, 2, 1, 3)
     return visibilities, series.reshape(2, 1, 2, quarters * spectra * channels)

time: 235 us -> 153 us (0.65)
  the two profiles are of different devices: /device:TPU:1 before, /device:TPU:38 now
where the time goes in v3:
time: 153 us
  Pallas kernels  139 us (91%)
  local copies, waits for them, and re-layouts  7.04 us (5%)
  waiting for transfers between devices  3.92 us (3%)
  starting transfers between devices  1.91 us (1%)
    pallas_call x1, Pallas kernels, turn(): pl.pallas_call(functools.partial(turn_kernel, quarters // 2, planes, acro...  92.7 us
    pallas_call x1, Pallas kernels, middle(): pl.pallas_call(middle_kernel, out_shape=(jax.ShapeDtypeStruct((2, channel...  34.8 us
    pallas_call x1, Pallas kernels, front(): pl.pallas_call(functools.partial(front_kernel, taps, channels), out_shape...  7.81 us
    unnamed x19, local copies, waits for them, and re-layouts  6.14 us
    pallas_call x1, Pallas kernels, tail(): pl.pallas_call(functools.partial(tail_kernel, taps, quarters), out_shape=...  3.95 us
    ppermute x1, waiting for transfers between devices, from_behind(): return lax.ppermute(block, axis, route)  3.92 us
  transfers between devices with their start and end apart: 1, of which 1 were waited for; matrix products, arithmetic and copies ran while one was open for 0% of the time, Pallas kernels for 0%

profile of v3, /device:TPU:38, one launch (start us, length us, event | category | flops | bytes accessed | tf_op | source)
XLA Modules:
  0.0 152.9 jit_solution(937616641701202527)
XLA Ops:
  0.6 0.0 copy-start.8
  0.6 0.9 slice.3
  1.5 1.9 %collective-permute-start = (bf16[2,16,1408]{2,1,0:T(8,128)(2,1)S(1)}, bf16[2,16,1408]{2,1,0:T(8,128)(2,1)S(1)}, u32[]{:S(2)}, u32[]{:S(2)}) collective-permute-start(bf16[2,16,1408]{2,1,0:T(8,128)(2,1)S(1)} %slice.3), channel_id=1, source_target_pairs={{0,1},{1,2},{2,3},{4,5},{5,6},{6,7},{8,9},{9,10},{10,11},{12,13},{... | collective-permute-start | bytes 270344 | tf_op jit(solution)/shard_map/ppermute | solution.py:404
  3.5 3.9 %collective-permute-done.h_ref = bf16[2,16,1408]{2,1,0:T(8,128)(2,1)S(1)} collective-permute-done((bf16[2,16,1408]{2,1,0:T(8,128)(2,1)S(1)}, bf16[2,16,1408]{2,1,0:T(8,128)(2,1)S(1)}, u32[]{:S(2)}, u32[]{:S(2)}) %collective-permute-start) | collective-permute-done | bytes 90144 | tf_op jit(solution)/shard_map/ppermute | solution.py:404
  7.4 0.0 copy-start
  7.4 1.6 %copy-done = bf16[2,16,32768]{2,1,0:T(8,128)(2,1)S(1)} copy-done((bf16[2,16,32768]{2,1,0:T(8,128)(2,1)S(1)}, bf16[2,16,32768]{2,1,0:T(8,128)(2,1)}, u32[]{:S(2)}) %copy-start) | copy-done | bytes 2097176
  9.0 0.0 copy-start.2
  9.0 0.9 copy-done.2
  9.9 0.0 copy-start.3
  9.9 0.9 copy-done.3
  10.8 0.7 copy-done.6
  11.5 7.8 %front.1 = bf16[4096,256]{1,0:T(8,128)(2,1)S(1)} custom-call(bf16[2,16,32768]{2,1,0:T(8,128)(2,1)S(1)} %copy-done, bf16[2,16,1408]{2,1,0:T(8,128)(2,1)S(1)} %collective-permute-done.h_ref, f32[12,128]{1,0:T(8,128)S(1)} %copy-done.6, bf16[256,256]{1,0:T(8,128)(2,1)S(1)} %copy-done.3, bf16[256,256]{1,0:T(8,128)(2,1)S(1)} %copy-done.2), custom_call_target="tpu_custom_call" | custom-call | tf_op jit(solution)/shard_map/front/pallas_call | solution.py:95
  19.3 0.0 copy-done.8
  19.3 0.0 copy-done.1
  19.3 92.7 %turn.1 = (bf16[4,2,2,1024,256]{4,3,2,1,0:T(8,128)(2,1)S(1)}, bf16[2,256,2048]{2,1,0:T(8,128)(2,1)S(1)}, bf16[1024,1024]{1,0:T(8,128)(2,1)S(1)}) custom-call(bf16[64,2,2,16,256]{4,3,2,1,0:T(8,128)(2,1)S(1)} %bitcast.8, bf16[2,2,128,1024]{3,2,1,0:T(8,128)(2,1)S(1)} %copy-done.1, s32[1,1024]{1,0:T(1,128)S(1)} %bitcast.10), custom_call_target="tpu_custom_call" | custom-call | tf_op jit(solution)/shard_map/turn/pallas_call | solution.py:248
  112.0 0.0 copy-start.4
  112.1 0.0 copy-start.5
  112.1 0.0 copy-start.7
  112.1 34.8 %middle.1 = (f32[2,2,256,1024]{3,2,1,0:T(8,128)S(1)}, bf16[64,2,16,256]{3,2,1,0:T(8,128)(2,1)S(1)}) custom-call(bf16[2,256,2048]{2,1,0:T(8,128)(2,1)S(1)} %get-tuple-element.7.weights_ref, bf16[4,2,2,1024,256]{4,3,2,1,0:T(8,128)(2,1)S(1)} %get-tuple-element.8.x_ref, bf16[1024,1024]{1,0:T(8,128)(2,1)S(1)} %get-tuple-element.9.pick_ref), custom_call_target="tpu_custom_call" | custom-call | tf_op jit(solution)/shard_map/middle/pallas_call | solution.py:330
  146.9 0.0 copy-done.4
  146.9 0.0 copy-done.5
  147.0 0.0 copy-done.7
  147.0 3.9 %tail.1 = f32[2,2048,128]{2,1,0:T(8,128)} custom-call(bf16[2048,256]{1,0:T(8,128)(2,1)S(1)} %bitcast.9, f32[12,128]{1,0:T(8,128)S(1)} %copy-done.7, bf16[256,256]{1,0:T(8,128)(2,1)S(1)} %copy-done.5, bf16[256,256]{1,0:T(8,128)(2,1)S(1)} %copy-done.4), custom_call_target="tpu_custom_call" | custom-call | tf_op jit(solution)/shard_map/tail/pallas_call | solution.py:390
  150.9 2.0 %copy.13 = f32[2,2,256,1024]{3,2,1,0:T(8,128)} copy(f32[2,2,256,1024]{3,2,1,0:T(8,128)S(1)} %get-tuple-element.14) | data formatting | bytes 8388608
  (2 shorter events, 0.0 us)
Async XLA Ops:
  0.6 18.7 %copy-start.8 = (s32[1024]{0:T(1024)S(1)}, s32[1024]{0:T(1024)}, u32[]{:S(2)}) copy-start(s32[1024]{0:T(1024)} %param.13) | copy-start | bytes 12292
  1.5 5.8 %collective-permute-start = (bf16[2,16,1408]{2,1,0:T(8,128)(2,1)S(1)}, bf16[2,16,1408]{2,1,0:T(8,128)(2,1)S(1)}, u32[]{:S(2)}, u32[]{:S(2)}) collective-permute-start(bf16[2,16,1408]{2,1,0:T(8,128)(2,1)S(1)} %slice.3), channel_id=1, source_target_pairs={{0,1},{1,2},{2,3},{4,5},{5,6},{6,7},{8,9},{9,10},{10,11},{12,13},{... | collective-permute-start | bytes 270344 | tf_op jit(solution)/shard_map/ppermute | solution.py:404
  7.4 1.6 %copy-start = (bf16[2,16,32768]{2,1,0:T(8,128)(2,1)S(1)}, bf16[2,16,32768]{2,1,0:T(8,128)(2,1)}, u32[]{:S(2)}) copy-start(bf16[2,16,32768]{2,1,0:T(8,128)(2,1)} %v_ref.1) | copy-start | bytes 6291460
  9.0 0.9 copy-start.2
  9.9 0.9 copy-start.3
  10.8 0.7 copy-start.6
  11.5 7.8 %copy-start.1 = (bf16[2,2,128,1024]{3,2,1,0:T(8,128)(2,1)S(1)}, bf16[2,2,128,1024]{3,2,1,0:T(8,128)(2,1)}, u32[]{:S(2)}) copy-start(bf16[2,2,128,1024]{3,2,1,0:T(8,128)(2,1)} %w_ref.1) | copy-start | bytes 3145732
  112.0 34.9 %copy-start.4 = (bf16[256,256]{1,0:T(8,128)(2,1)S(1)}, bf16[256,256]{1,0:T(8,128)(2,1)}, u32[]{:S(2)}) copy-start(bf16[256,256]{1,0:T(8,128)(2,1)} %constant.11.clone.low_ref) | copy-start | bytes 393220
  112.1 34.9 %copy-start.5 = (bf16[256,256]{1,0:T(8,128)(2,1)S(1)}, bf16[256,256]{1,0:T(8,128)(2,1)}, u32[]{:S(2)}) copy-start(bf16[256,256]{1,0:T(8,128)(2,1)} %constant.10.clone.high_ref) | copy-start | bytes 393220
  112.1 34.9 %copy-start.7 = (f32[12,128]{1,0:T(8,128)S(1)}, f32[12,128]{1,0:T(8,128)}, u32[]{:S(2)}) copy-start(f32[12,128]{1,0:T(8,128)} %taps_ref.3) | copy-start | bytes 18436

commit v4 on v3

--- a/solution.py
+++ b/solution.py
@@ -122,7 +122,7 @@
 
 def turn_kernel(
     sides, planes, across, s_ref, w_ref, order_ref, x_ref, weights_ref, pick_ref,
-    relay_ref, send, arrive, relayed, onward, forward, forwarded, share, shared,
+    send, arrive, forward, forwarded, share, shared,
 ):
     pairs_count = lax.axis_size("stn") // planes
     stn, beam = lax.axis_index("stn"), lax.axis_index("beam")
@@ -140,42 +140,43 @@
         first = pl.multiple_of((pair * planes + ((x + across - dx) % across) * across) * rows, across * rows)
         return ref.at[:, :, pl.ds(first, across * rows), :]
 
-    def entering(at, dx):
+    def entering(at, dx, groups):
         border = (p + 3 + 2 * at) % pairs_count
-        for group, pair, start in ((1, border, at), (3, far, 1 - at), (2, border, 1 - at), (0, p, at)):
+        for group in groups:
+            pair, start = ((p, at), (border, at), (border, 1 - at), (far, 1 - at))[group]
             yield group, part(x_ref.at[start * 2 + core], pair, dx), start
 
     hail(sibling)
+    hail(partner)
 
     @pl.loop(0, planes)
     def _(i):
-        for pair, to in ((p, others), (near, others), (far, others)):
+        for pair, to in ((near, mine), (near, others), (far, others)):
             hail((pair * planes + i, to))
 
         @pl.when(i != place)
         def _():
             hail((p * planes + i, mine))
 
-    pl.semaphore_wait(pltpu.get_barrier_semaphore(), 4 * planes)
+    pl.semaphore_wait(pltpu.get_barrier_semaphore(), 4 * planes + 1)
 
     first = pl.multiple_of(stn * rows, rows)
     landing = x_ref.at[mine, :, :, pl.ds(first, rows), :]
+    pltpu.make_async_copy(s_ref.at[stn], landing, arrive.at[0, 0]).start()
+
+    def depart(group, dx, dy):
+        pair, entry = ((p, mine), (beyond, mine), (near, others), (far, others))[group]
+        owner = pair * planes + ((x + dx) % across) * across + (y + dy) % across
+        remote(s_ref.at[owner], landing, send, arrive.at[group, dx], (owner, entry)).start()
+
+    @pl.loop(1, planes)
+    def _(i):
+        depart(0, i // across, i % across)
 
     @pl.loop(0, planes)
     def _(i):
-        dx, dy = i // across, i % across
-        goal = ((x + dx) % across) * across + (y + dy) % across
-        remote(s_ref.at[beyond * planes + goal], relay_ref.at[place], send, relayed.at[dx], (p * planes + goal, others)).start()
-        remote(s_ref.at[far * planes + goal], landing, send, arrive.at[3, dx], (far * planes + goal, others)).start()
-        remote(s_ref.at[near * planes + goal], landing, send, arrive.at[2, dx], (near * planes + goal, others)).start()
-
-        @pl.when(i != 0)
-        def _():
-            remote(s_ref.at[p * planes + goal], landing, send, arrive.at[0, dx], (p * planes + goal, mine)).start()
-
-        @pl.when(i == 0)
-        def _():
-            pltpu.make_async_copy(s_ref.at[stn], landing, arrive.at[0, 0]).start()
+        for group in (3, 1, 2):
+            depart(group, i // across, i % across)
 
     stations = order_ref.shape[1]
 
@@ -185,55 +186,50 @@
         station = lax.broadcasted_iota(jnp.int32, (64, stations), 0) + first
         pick_ref[pl.ds(first, 64), :] = jnp.where(order_ref[...] == station, 1.0, 0.0).astype(BF16)
 
-    def relay(dx):
-        block = relay_ref.at[pl.ds(((x + across - dx) % across) * across, across)]
-        wait(block, relayed.at[dx])
-        for i in range(across):
-            source = (x + across - dx) % across * across + i
-            first = pl.multiple_of((p * planes + source) * rows, rows)
-            goal = x_ref.at[others, :, :, pl.ds(first, rows), :]
-            remote(relay_ref.at[source], goal, onward, arrive.at[1, dx], (near * planes + place, others)).start()
-
-    def entered(dx):
-        for group, block, start in entering(side, dx):
+    def entered(groups, dx):
+        for group, block, start in entering(side, dx, groups):
             wait(block, arrive.at[group, dx])
             remote(block, block, forward, forwarded.at[group, dx], partner).start()
             remote(block, block, share.at[start], shared.at[start], sibling).start()
 
-    def passed(dx):
-        for group, block, start in entering(1 - side, dx):
+    def passed(groups, dx):
+        for group, block, start in entering(1 - side, dx, groups):
             wait(block, forwarded.at[group, dx])
             remote(block, block, share.at[start], shared.at[start], sibling).start()
 
-    @pl.loop(0, across + 2)
+    def weigh(c):
+        half = w_ref.shape[2]
+        both = jnp.concatenate([w_ref[0, c], w_ref[1, c]], axis=0)
+        for at in range(0, stations, 256):
+            turned = dot(both, pick_ref[:, at : at + 256], ((1,), (0,)))
+            weights_ref[c, :, at : at + 256] = turned.astype(BF16)
+            crossed = jnp.concatenate([-turned[half:], turned[:half]], axis=0)
+            weights_ref[c, :, stations + at : stations + at + 256] = crossed.astype(BF16)
+
+    @pl.loop(0, across)
+    def _(dx):
+        entered((0,), dx)
+
+    @pl.loop(0, across)
     def _(step):
-        @pl.when(step < across)
-        def _():
-            relay(step)
-
-        @pl.when((step > 0) & (step <= across))
-        def _():
-            entered(step - 1)
-
-        @pl.when(step > 1)
-        def _():
-            passed(step - 2)
+        entered((2, 1, 3), step)
 
         @pl.when(step < w_ref.shape[1])
         def _():
-            both = jnp.concatenate([w_ref[0, step], w_ref[1, step]], axis=0)
-            half = w_ref.shape[2]
-            for at in range(0, stations, 256):
-                turned = dot(both, pick_ref[:, at : at + 256], ((1,), (0,)))
-                weights_ref[step, :, at : at + 256] = turned.astype(BF16)
-                crossed = jnp.concatenate([-turned[half:], turned[:half]], axis=0)
-                weights_ref[step, :, stations + at : stations + at + 256] = crossed.astype(BF16)
+            weigh(step)
+
+        passed((0,), step)
+
+        @pl.when(step > 0)
+        def _():
+            passed((2, 1, 3), step - 1)
+
+    passed((2, 1, 3), across - 1)
 
     for start in range(sides):
         wait(x_ref.at[start * 2 + 1 - core], shared.at[start])
         wait(x_ref.at[start * 2 + core], share.at[start])
     wait(x_ref.at[0], forward)
-    wait(relay_ref, onward)
     wait(s_ref.at[pl.ds(0, 4 * planes - 1)], send)
 
 
@@ -255,8 +251,7 @@
         in_specs=[vmem] * 3,
         out_specs=(vmem,) * 3,
         scratch_shapes=[
-            pltpu.VMEM((planes, channels, parts, rows, spectra), BF16),
-            dma, dma((4, across)), dma((across,)), dma, dma, dma((4, across)), dma((2,)), dma((2,)),
+            dma, dma((4, across)), dma, dma((4, across)), dma((2,)), dma((2,)),
         ],
         compiler_params=pltpu.CompilerParams(collective_id=0, has_side_effects=True, vmem_limit_bytes=28 * MIB),
         name="turn",
@@ -347,7 +342,11 @@
     )(weights, x, pick)
 
 
-def tail_kernel(taps, quarters, g_ref, taps_ref, high_ref, low_ref, out_ref, left_ref, right_ref, *lines):
+def tail_kernel(
+    taps, quarters, g_ref, vis_ref, taps_ref, high_ref, low_ref, out_ref, kept_ref, saved, left_ref, right_ref, *lines
+):
+    save = pltpu.make_async_copy(vis_ref, kept_ref, saved)
+    save.start()
     channels = high_ref.shape[0] // 2
     spectra = g_ref.shape[1]
     pad = 16
@@ -379,9 +378,10 @@
                 for m in range(1, taps):
                     total += weights[m] * line[pad + t - m : pad + t - m + block, :]
                 out_ref[part, pl.ds(2 * t + j, block, stride=2), :] = total
-
-
-def tail(arrived, synth_taps, quarters):
+    save.wait()
+
+
+def tail(arrived, visibilities, synth_taps, quarters):
     taps, channels = synth_taps.shape
     rows, spectra = arrived.shape
     high, low = split(spin_matrix(channels).T)
@@ -389,13 +389,17 @@
     total = quarters * spectra
     return pl.pallas_call(
         functools.partial(tail_kernel, taps, quarters),
-        out_shape=jax.ShapeDtypeStruct((2, 2 * total, channels), F32),
-        in_specs=[vmem] * 4,
-        out_specs=vmem,
-        scratch_shapes=[pltpu.VMEM((rows, 128), F32)] * 2 + [pltpu.VMEM((total + 16, channels), F32)] * 4,
+        out_shape=(
+            jax.ShapeDtypeStruct((2, 2 * total, channels), F32),
+            jax.ShapeDtypeStruct(visibilities.shape, F32),
+        ),
+        in_specs=[vmem] * 5,
+        out_specs=(vmem, pl.BlockSpec(memory_space=pl.ANY)),
+        scratch_shapes=[pltpu.SemaphoreType.DMA]
+        + [pltpu.VMEM((rows, 128), F32)] * 2 + [pltpu.VMEM((total + 16, channels), F32)] * 4,
         compiler_params=pltpu.CompilerParams(vmem_limit_bytes=40 * MIB),
         name="tail",
-    )(arrived, synth_taps, high, low)
+    )(arrived, visibilities, synth_taps, high, low)
 
 
 def from_behind(block, axis, distance):
@@ -417,7 +421,7 @@
     spectral = front(voltages, history, filter_taps).reshape(owners, held, 2, rows, spectra)
     x, weights, pick = turn(spectral, beam_weights, station_order)
     visibilities, arrived = middle(weights, x, pick)
-    series = tail(arrived.reshape(-1, spectra), synth_taps, quarters)
+    series, visibilities = tail(arrived.reshape(-1, spectra), visibilities, synth_taps, quarters)
     series = series.reshape(2, quarters * spectra, 2, channels).transpose(0, 2, 1, 3)
     return visibilities, series.reshape(2, 1, 2, quarters * spectra * channels)
 

time: 153 us -> 139 us (0.908)
  the two profiles are of different devices: /device:TPU:38 before, /device:TPU:6 now
where the time goes in v4:
time: 139 us; the launch traced here: 138 us
  Pallas kernels  130 us (94%)
  local copies, waits for them, and re-layouts  5.03 us (4%)
  starting transfers between devices  1.73 us (1%)
    pallas_call x1, Pallas kernels, turn(): pl.pallas_call(functools.partial(turn_kernel, quarters // 2, planes, acro...  83.3 us
    pallas_call x1, Pallas kernels, middle(): pl.pallas_call(middle_kernel, out_shape=(jax.ShapeDtypeStruct((2, channel...  34.7 us
    pallas_call x1, Pallas kernels, front(): pl.pallas_call(functools.partial(front_kernel, taps, channels), out_shape...  7.82 us
    unnamed x18, local copies, waits for them, and re-layouts  4.12 us
    pallas_call x1, Pallas kernels, tail(): pl.pallas_call(functools.partial(tail_kernel, taps, quarters), out_shape=...  3.92 us
  transfers between devices with their start and end apart: 1, of which 1 were waited for; matrix products, arithmetic and copies ran while one was open for 0% of the time, Pallas kernels for 0%

profile of v4, /device:TPU:6, one launch (start us, length us, event | category | flops | bytes accessed | tf_op | source)
XLA Modules:
  0.0 138.3 jit_solution(59468866717479112)
XLA Ops:
  0.6 0.0 copy-start.8
  0.6 0.9 slice.3
  1.5 1.7 %collective-permute-start = (bf16[2,16,1408]{2,1,0:T(8,128)(2,1)S(1)}, bf16[2,16,1408]{2,1,0:T(8,128)(2,1)S(1)}, u32[]{:S(2)}, u32[]{:S(2)}) collective-permute-start(bf16[2,16,1408]{2,1,0:T(8,128)(2,1)S(1)} %slice.3), channel_id=1, source_target_pairs={{0,1},{1,2},{2,3},{4,5},{5,6},{6,7},{8,9},{9,10},{10,11},{12,13},{... | collective-permute-start | bytes 270344 | tf_op jit(solution)/shard_map/ppermute | solution.py:408
  3.3 0.9 collective-permute-done.h_ref
  4.2 0.0 copy-start
  4.2 1.6 %copy-done = bf16[2,16,32768]{2,1,0:T(8,128)(2,1)S(1)} copy-done((bf16[2,16,32768]{2,1,0:T(8,128)(2,1)S(1)}, bf16[2,16,32768]{2,1,0:T(8,128)(2,1)}, u32[]{:S(2)}) %copy-start) | copy-done | bytes 2097176
  5.8 0.0 copy-start.4
  5.8 0.9 copy-done.4
  6.7 0.0 copy-start.5
  6.7 0.9 copy-done.5
  7.6 0.0 copy-start.6
  7.6 0.7 copy-done.6
  8.3 7.8 %front.1 = bf16[4096,256]{1,0:T(8,128)(2,1)S(1)} custom-call(bf16[2,16,32768]{2,1,0:T(8,128)(2,1)S(1)} %copy-done, bf16[2,16,1408]{2,1,0:T(8,128)(2,1)S(1)} %collective-permute-done.h_ref, f32[12,128]{1,0:T(8,128)S(1)} %copy-done.6, bf16[256,256]{1,0:T(8,128)(2,1)S(1)} %copy-done.5, bf16[256,256]{1,0:T(8,128)(2,1)S(1)} %copy-done.4), custom_call_target="tpu_custom_call" | custom-call | tf_op jit(solution)/shard_map/front/pallas_call | solution.py:95
  16.1 0.0 copy-done.8
  16.1 0.0 copy-done.1
  16.1 83.3 %turn.1 = (bf16[4,2,2,1024,256]{4,3,2,1,0:T(8,128)(2,1)S(1)}, bf16[2,256,2048]{2,1,0:T(8,128)(2,1)S(1)}, bf16[1024,1024]{1,0:T(8,128)(2,1)S(1)}) custom-call(bf16[64,2,2,16,256]{4,3,2,1,0:T(8,128)(2,1)S(1)} %bitcast.8, bf16[2,2,128,1024]{3,2,1,0:T(8,128)(2,1)S(1)} %copy-done.1, s32[1,1024]{1,0:T(1,128)S(1)} %bitcast.10), custom_call_target="tpu_custom_call" | custom-call | tf_op jit(solution)/shard_map/turn/pallas_call | solution.py:244
  99.5 0.0 copy-start.2
  99.5 0.0 copy-start.3
  99.5 0.0 copy-start.7
  99.5 34.7 %middle.1 = (f32[2,2,256,1024]{3,2,1,0:T(8,128)S(1)}, bf16[64,2,16,256]{3,2,1,0:T(8,128)(2,1)S(1)}) custom-call(bf16[2,256,2048]{2,1,0:T(8,128)(2,1)S(1)} %get-tuple-element.9.weights_ref, bf16[4,2,2,1024,256]{4,3,2,1,0:T(8,128)(2,1)S(1)} %get-tuple-element.10.x_ref, bf16[1024,1024]{1,0:T(8,128)(2,1)S(1)} %get-tuple-element.11.pick_ref), custom_call_target="tpu_custom_call" | custom-call | tf_op jit(solution)/shard_map/middle/pallas_call | solution.py:325
  134.2 0.0 copy-done.2
  134.2 0.0 copy-done.3
  134.3 0.0 copy-done.7
  134.3 3.9 %tail.1 = (f32[2,2048,128]{2,1,0:T(8,128)}, f32[2,2,256,1024]{3,2,1,0:T(8,128)}) custom-call(bf16[2048,256]{1,0:T(8,128)(2,1)S(1)} %bitcast.9, f32[2,2,256,1024]{3,2,1,0:T(8,128)S(1)} %get-tuple-element.13.vis_ref, f32[12,128]{1,0:T(8,128)S(1)} %copy-done.7, bf16[256,256]{1,0:T(8,128)(2,1)S(1)} %copy-done.3, bf16[256,256]{1,0:T(8,128)(2,1)S(1)} %copy-done.2), custom_call_target="tpu_custom_call" | custom-call | tf_op jit(solution)/shard_map/tail/pallas_call | solution.py:390
  (1 shorter events, 0.0 us)
Async XLA Ops:
  0.6 15.5 %copy-start.8 = (s32[1024]{0:T(1024)S(1)}, s32[1024]{0:T(1024)}, u32[]{:S(2)}) copy-start(s32[1024]{0:T(1024)} %param.13) | copy-start | bytes 12292
  1.5 2.7 %collective-permute-start = (bf16[2,16,1408]{2,1,0:T(8,128)(2,1)S(1)}, bf16[2,16,1408]{2,1,0:T(8,128)(2,1)S(1)}, u32[]{:S(2)}, u32[]{:S(2)}) collective-permute-start(bf16[2,16,1408]{2,1,0:T(8,128)(2,1)S(1)} %slice.3), channel_id=1, source_target_pairs={{0,1},{1,2},{2,3},{4,5},{5,6},{6,7},{8,9},{9,10},{10,11},{12,13},{... | collective-permute-start | bytes 270344 | tf_op jit(solution)/shard_map/ppermute | solution.py:408
  4.2 1.6 %copy-start = (bf16[2,16,32768]{2,1,0:T(8,128)(2,1)S(1)}, bf16[2,16,32768]{2,1,0:T(8,128)(2,1)}, u32[]{:S(2)}) copy-start(bf16[2,16,32768]{2,1,0:T(8,128)(2,1)} %v_ref.1) | copy-start | bytes 6291460
  5.8 0.9 copy-start.4
  6.7 0.9 copy-start.5
  7.6 0.7 copy-start.6
  8.3 7.8 %copy-start.1 = (bf16[2,2,128,1024]{3,2,1,0:T(8,128)(2,1)S(1)}, bf16[2,2,128,1024]{3,2,1,0:T(8,128)(2,1)}, u32[]{:S(2)}) copy-start(bf16[2,2,128,1024]{3,2,1,0:T(8,128)(2,1)} %w_ref.1) | copy-start | bytes 3145732
  99.5 34.8 %copy-start.2 = (bf16[256,256]{1,0:T(8,128)(2,1)S(1)}, bf16[256,256]{1,0:T(8,128)(2,1)}, u32[]{:S(2)}) copy-start(bf16[256,256]{1,0:T(8,128)(2,1)} %constant.11.clone.low_ref) | copy-start | bytes 393220
  99.5 34.8 %copy-start.3 = (bf16[256,256]{1,0:T(8,128)(2,1)S(1)}, bf16[256,256]{1,0:T(8,128)(2,1)}, u32[]{:S(2)}) copy-start(bf16[256,256]{1,0:T(8,128)(2,1)} %constant.10.clone.high_ref) | copy-start | bytes 393220
  99.5 34.8 %copy-start.7 = (f32[12,128]{1,0:T(8,128)S(1)}, f32[12,128]{1,0:T(8,128)}, u32[]{:S(2)}) copy-start(f32[12,128]{1,0:T(8,128)} %taps_ref.3) | copy-start | bytes 18436

commit v5 on v4

v5 whole, which is shorter than its diff:
```python
import functools
import math

import jax
import jax.numpy as jnp
import numpy as np
from jax import lax
from jax.experimental import pallas as pl
from jax.experimental.pallas import tpu as pltpu
from jax.sharding import PartitionSpec as P

F32, BF16 = jnp.float32, jnp.bfloat16
MIB = 2**20


def spin_matrix(points):
    index = np.arange(points)
    angles = (index[:, None] * index[None, :] % points) * (2.0 * math.pi / points)
    cosine, sine = np.cos(angles) / math.sqrt(points), np.sin(angles) / math.sqrt(points)
    upper = np.concatenate([cosine, -sine], axis=1)
    lower = np.concatenate([sine, cosine], axis=1)
    return np.concatenate([upper, lower], axis=0).astype(np.float32)


def split(matrix):
    high = matrix.astype(jnp.bfloat16)
    low = (matrix - high.astype(np.float32)).astype(jnp.bfloat16)
    return jnp.asarray(high), jnp.asarray(low)


def dot(a, b, dims):
    return lax.dot_general(a, b, (dims, ((), ())), preferred_element_type=F32)


MESH = pl.DeviceIdType.MESH


def remote(source, goal, out, into, device):
    return pltpu.make_async_remote_copy(
        src_ref=source, dst_ref=goal, send_sem=out, recv_sem=into, device_id=device, device_id_type=MESH
    )


def wait(ref, sem):
    pltpu.make_async_copy(ref, ref, sem).wait()


def hail(device):
    pl.semaphore_signal(pltpu.get_barrier_semaphore(), inc=1, device_id=device, device_id_type=MESH)


def fir(taps, tile, weights, t0, store):
    step, rows = 8, weights[0].shape[0]
    tiles = [tile(i - (taps - 1)) for i in range(step + taps - 1)]
    for j in range(step):
        total = weights[0] * tiles[j + taps - 1]
        for m in range(1, taps):
            total += weights[m] * tiles[j + taps - 1 - m]
        store[pl.ds((t0 + j) * rows, rows), :] = total


def main_kernel(
    sides, planes, across, v_hbm, w_hbm, taps_hbm, high_hbm, low_hbm, order_ref, vis_hbm, got_ref,
    v_ref, w_ref, taps_ref, high_ref, low_ref, rim_ref, re_ref, im_ref, left_ref, right_ref, s_ref, x_ref, weights_ref,
    pick_ref, formed_ref, turned_ref, vis_ref, loads, saves, rim_send, rim_arrive, send, arrive, forward, forwarded, share, shared,
    beam_send, beam_arrive,
):
    owners = lax.axis_size("stn")
    pairs_count = owners // planes
    stn, beam = lax.axis_index("stn"), lax.axis_index("beam")
    p, place = stn // planes, stn % planes
    x, y = place // across, place % across
    side, core = beam // 2, beam % 2
    quarters, channels, _, stations, spectra = x_ref.shape
    rows = s_ref.shape[3]
    taps, points = taps_ref.shape
    mine, others = side * 2 + core, (1 - side) * 2 + core
    partner, sibling = (stn, others), (stn, side * 2 + 1 - core)
    later, sooner = (stn, (beam + 1) % quarters), (stn, (beam + quarters - 1) % quarters)
    near = (p + 3 + 2 * side) % pairs_count
    far = (p + 2) % pairs_count
    beyond = (p + 1 + 2 * side) % pairs_count
    nn, nt = ((1,), (0,)), ((1,), (1,))

    pieces = ((v_hbm, v_ref), (taps_hbm, taps_ref), (high_hbm, high_ref), (low_hbm, low_ref), (w_hbm, w_ref))
    fetches = [pltpu.make_async_copy(a, b, loads.at[i]) for i, (a, b) in enumerate(pieces)]
    for fetch in fetches:
        fetch.start()

    hail(sibling)
    hail(partner)
    hail(sooner)

    @pl.loop(1, owners)
    def _(i):
        hail(((stn + i) % owners, beam))

    @pl.loop(0, planes)
    def _(i):
        hail((near * planes + i, others))
        hail((far * planes + i, others))

    fetches[0].wait()
    fetches[1].wait()
    filters = [jnp.broadcast_to(taps_ref[m : m + 1, :], (rows, points)) for m in range(taps)]
    stores = (re_ref, im_ref)

    @pl.loop(2, spectra // 8)
    def _(block):
        for part in range(2):

            def tile(i, part=part):
                return v_ref[part, :, pl.ds(pl.multiple_of((block * 8 + i) * points, points), points)].astype(F32)

            fir(taps, tile, filters, block * 8, stores[part])

    pl.semaphore_wait(pltpu.get_barrier_semaphore(), owners - 1 + 2 * planes + 3)
    rim = (taps - 1) * points
    remote(v_ref.at[:, :, pl.ds((spectra - taps + 1) * points, rim)], rim_ref, rim_send, rim_arrive, later).start()

    @pl.loop(0, stations // 64)
    def _(i):
        first = pl.multiple_of(i * 64, 64)
        station = lax.broadcasted_iota(jnp.int32, (64, stations), 0) + first
        pick_ref[pl.ds(first, 64), :] = jnp.where(order_ref[...] == station, 1.0, 0.0).astype(BF16)

    wait(rim_ref, rim_arrive)
    for block in range(2):
        for part in range(2):

            def tile(i, block=block, part=part):
                t = block * 8 + i
                if t >= 0:
                    return v_ref[part, :, t * points : (t + 1) * points].astype(F32)
                t += taps - 1
                before = rim_ref[part, :, t * points : (t + 1) * points].astype(F32)
                return jnp.where(beam > 0, before, jnp.zeros_like(before))

            fir(taps, tile, filters, block * 8, stores[part])

    fetches[2].wait()
    fetches[3].wait()
    lines = 2 * points
    for i in range(rows):
        at = pl.ds(i, spectra, stride=rows)
        wide = jnp.concatenate([re_ref[at, :], im_ref[at, :]], axis=1)
        high = wide.astype(BF16)
        low = (wide - high.astype(F32)).astype(BF16)
        result = dot(high_ref[...], high, nt) + dot(high_ref[...], low, nt) + dot(low_ref[...], high, nt)
        left_ref[pl.ds(i, lines, stride=rows), :] = result[:, :128]
        right_ref[pl.ds(i, lines, stride=rows), :] = result[:, 128:]

    @pl.loop(0, owners // 4)
    def _(i):
        count = channels * 2 * rows
        for j in range(4):
            at = pl.ds(pl.multiple_of((i * 4 + j) * count, count), count)
            s_ref[i * 4 + j, :, :, :, :128] = left_ref[at, :].astype(BF16).reshape(channels, 2, rows, 128)
            s_ref[i * 4 + j, :, :, :, 128:] = right_ref[at, :].astype(BF16).reshape(channels, 2, rows, 128)

    def entering(at, dx, groups):
        border = (p + 3 + 2 * at) % pairs_count
        for group in groups:
            pair, start = ((p, at), (border, at), (border, 1 - at), (far, 1 - at))[group]
            first = pl.multiple_of((pair * planes + ((x + across - dx) % across) * across) * rows, across * rows)
            yield group, x_ref.at[start * 2 + core, :, :, pl.ds(first, across * rows), :], start

    landing = x_ref.at[mine, :, :, pl.ds(pl.multiple_of(stn * rows, rows), rows), :]
    pltpu.make_async_copy(s_ref.at[stn], landing, arrive.at[0, 0]).start()

    def depart(group, dx, dy):
        pair, entry = ((p, mine), (beyond, mine), (near, others), (far, others))[group]
        owner = pair * planes + ((x + dx) % across) * across + (y + dy) % across
        remote(s_ref.at[owner], landing, send, arrive.at[group, dx], (owner, entry)).start()

    @pl.loop(1, planes)
    def _(i):
        depart(0, i // across, i % across)

    @pl.loop(0, planes)
    def _(i):
        for group in (3, 1, 2):
            depart(group, i // across, i % across)

    def entered(groups, dx):
        for group, block, start in entering(side, dx, groups):
            wait(block, arrive.at[group, dx])
            remote(block, block, forward, forwarded.at[group, dx], partner).start()
            remote(block, block, share.at[start], shared.at[start], sibling).start()

    def passed(groups, dx):
        for group, block, start in entering(1 - side, dx, groups):
            wait(block, forwarded.at[group, dx])
            remote(block, block, share.at[start], shared.at[start], sibling).start()

    half = w_ref.shape[2]

    def weigh(c):
        both = jnp.concatenate([w_ref[0, c], w_ref[1, c]], axis=0)
        for at in range(0, stations, 256):
            turned = dot(both, pick_ref[:, at : at + 256], nn)
            weights_ref[c, :, at : at + 256] = turned.astype(BF16)
            crossed = jnp.concatenate([-turned[half:], turned[:half]], axis=0)
            weights_ref[c, :, stations + at : stations + at + 256] = crossed.astype(BF16)

    @pl.loop(0, across)
    def _(dx):
        entered((0,), dx)

    fetches[4].wait()

    @pl.loop(0, across)
    def _(step):
        entered((2, 1, 3), step)

        @pl.when(step < channels)
        def _():
            weigh(step)

        passed((0,), step)

        @pl.when(step > 0)
        def _():
            passed((2, 1, 3), step - 1)

    passed((2, 1, 3), across - 1)
    for start in range(sides):
        wait(x_ref.at[start * 2 + 1 - core], shared.at[start])

    @pl.loop(0, channels)
    def _(c):
        @pl.loop(0, quarters)
        def _(q):
            result = dot(weights_ref[c, :, :stations], x_ref[q, c, 0], nn)
            result += dot(weights_ref[c, :, stations:], x_ref[q, c, 1], nn)
            for part in range(2):
                beams = result[part * half : (part + 1) * half]
                left_ref[pl.ds(q * 2 + part, half, stride=8), :] = beams[:, :128]
                right_ref[pl.ds(q * 2 + part, half, stride=8), :] = beams[:, 128:]

        for d in range(0, owners, 8):
            at = slice(d * 16, (d + 8) * 16)
            formed_ref[c, d : d + 8, :, :128] = left_ref[at, :].astype(BF16).reshape(8, 16, 128)
            formed_ref[c, d : d + 8, :, 128:] = right_ref[at, :].astype(BF16).reshape(8, 16, 128)

        pltpu.make_async_copy(formed_ref.at[c, stn], got_ref.at[c, stn], beam_arrive.at[c]).start()

        @pl.loop(1, owners)
        def _(i):
            owner = (stn + i) % owners
            remote(formed_ref.at[c, owner], got_ref.at[c, stn], beam_send.at[c], beam_arrive.at[c], (owner, beam)).start()

    count = vis_ref.shape[2]
    start = pl.multiple_of(beam * count, count)
    scale = 1.0 / (quarters * spectra)

    @pl.loop(0, channels)
    def _(c):
        for q in range(quarters):
            at = slice(q * spectra, (q + 1) * spectra)
            for part in range(2):
                for r in range(0, stations, 256):
                    turned_ref[part, r : r + 256, at] = dot(pick_ref[r : r + 256, :], x_ref[q, c, part], nn).astype(BF16)
        real_rows = turned_ref[0, pl.ds(start, count), :]
        imag_rows = turned_ref[1, pl.ds(start, count), :]
        for at in range(0, stations, 256):
            cols = slice(at, at + 256)
            real, imag = turned_ref[0, cols, :], turned_ref[1, cols, :]
            vis_ref[0, c, :, cols] = (dot(real_rows, real, nt) + dot(imag_rows, imag, nt)) * scale
            vis_ref[1, c, :, cols] = (dot(imag_rows, real, nt) - dot(real_rows, imag, nt)) * scale
        pltpu.make_async_copy(vis_ref.at[:, c], vis_hbm.at[:, c], saves.at[c]).start()

    for start in range(sides):
        wait(x_ref.at[start * 2 + core], share.at[start])
    wait(x_ref.at[0], forward)
    wait(s_ref.at[pl.ds(0, owners - 1)], send)
    wait(rim_ref, rim_send)
    for c in range(channels):
        wait(vis_ref.at[:, c], saves.at[c])
        wait(got_ref.at[c], beam_arrive.at[c])
        wait(formed_ref.at[c, pl.ds(0, owners - 1)], beam_send.at[c])


def main(voltages, beam_weights, filter_taps, station_order):
    quarters, owners = lax.axis_size("beam"), lax.axis_size("stn")
    taps, points = filter_taps.shape
    rows, spectra = voltages.shape[1], voltages.shape[2] // points
    channels, half, stations = beam_weights.shape[1:]
    across = 4
    order = np.array([ri * points + c for c in range(points) for ri in range(2)])
    high, low = split(spin_matrix(points).T[order])
    dma = pltpu.SemaphoreType.DMA
    vmem, anywhere = pl.BlockSpec(memory_space=pltpu.VMEM), pl.BlockSpec(memory_space=pl.ANY)
    return pl.pallas_call(
        functools.partial(main_kernel, quarters // 2, across * across, across),
        out_shape=(
            jax.ShapeDtypeStruct((2, channels, stations // quarters, stations), F32),
            jax.ShapeDtypeStruct((channels, owners, 16, spectra), BF16),
        ),
        in_specs=[anywhere] * 5 + [vmem],
        out_specs=(anywhere, anywhere),
        scratch_shapes=[
            pltpu.VMEM(voltages.shape, BF16),
            pltpu.VMEM(beam_weights.shape, BF16),
            pltpu.VMEM(filter_taps.shape, F32),
            pltpu.VMEM(high.shape, BF16),
            pltpu.VMEM(low.shape, BF16),
            pltpu.VMEM((2, rows, (taps - 1) * points), BF16),
            pltpu.VMEM((spectra * rows, points), F32),
            pltpu.VMEM((spectra * rows, points), F32),
            pltpu.VMEM((2 * points * rows, 128), F32),
            pltpu.VMEM((2 * points * rows, 128), F32),
            pltpu.VMEM((owners, channels, 2, rows, spectra), BF16),
            pltpu.VMEM((quarters, channels, 2, stations, spectra), BF16),
            pltpu.VMEM((channels, 2 * half, 2 * stations), BF16),
            pltpu.VMEM((stations, stations), BF16),
            pltpu.VMEM((channels, owners, 16, spectra), BF16),
            pltpu.VMEM((2, stations, quarters * spectra), BF16),
            pltpu.VMEM((2, channels, stations // quarters, stations), F32),
            dma((5,)), dma((channels,)), dma, dma, dma, dma((4, across)), dma, dma((4, across)), dma((2,)), dma((2,)),
            dma((channels,)), dma((channels,)),
        ],
        compiler_params=pltpu.CompilerParams(collective_id=0, has_side_effects=True, vmem_limit_bytes=54 * MIB),
        name="main",
    )(voltages, beam_weights, filter_taps, high, low, station_order.reshape(1, stations))


def tail_kernel(
    taps, quarters, g_ref, vis_ref, taps_ref, high_ref, low_ref, out_ref, kept_ref, saved, left_ref, right_ref, *lines
):
    save = pltpu.make_async_copy(vis_ref, kept_ref, saved)
    save.start()
    channels = high_ref.shape[0] // 2
    spectra = g_ref.shape[1]
    pad = 16
    left_ref[...] = g_ref[:, :128].astype(F32)
    right_ref[...] = g_ref[:, 128:].astype(F32)
    tn = ((0,), (0,))
    for line in lines:
        line[:pad, :] = jnp.zeros((pad, channels), F32)
    for j in range(2):
        for q in range(quarters):
            parts = [
                jnp.concatenate(
                    [ref[pl.ds(j * 8 + q * 2 + ri, channels, stride=16), :] for ref in (left_ref, right_ref)], axis=1
                )
                for ri in range(2)
            ]
            both = jnp.concatenate(parts, axis=0).astype(BF16)
            result = dot(both, high_ref[...], tn) + dot(both, low_ref[...], tn)
            at = slice(pad + q * spectra, pad + (q + 1) * spectra)
            lines[2 * j][at, :] = result[:, :channels]
            lines[2 * j + 1][at, :] = result[:, channels:]
    block = 64
    weights = [jnp.broadcast_to(taps_ref[m : m + 1, :], (block, channels)) for m in range(taps)]
    for j in range(2):
        for part in range(2):
            line = lines[2 * j + part]
            for t in range(0, quarters * spectra, block):
                total = weights[0] * line[pad + t : pad + t + block, :]
                for m in range(1, taps):
                    total += weights[m] * line[pad + t - m : pad + t - m + block, :]
                out_ref[part, pl.ds(2 * t + j, block, stride=2), :] = total
    save.wait()


def tail(arrived, visibilities, synth_taps, quarters, owners):
    taps, channels = synth_taps.shape
    rows, spectra = arrived.shape
    order = np.arange(2 * channels).reshape(2, owners, channels // owners).transpose(0, 2, 1).reshape(-1)
    high, low = split(spin_matrix(channels).T[order])
    vmem = pl.BlockSpec(memory_space=pltpu.VMEM)
    total = quarters * spectra
    return pl.pallas_call(
        functools.partial(tail_kernel, taps, quarters),
        out_shape=(
            jax.ShapeDtypeStruct((2, 2 * total, channels), F32),
            jax.ShapeDtypeStruct(visibilities.shape, F32),
        ),
        in_specs=[vmem, pl.BlockSpec(memory_space=pl.ANY), vmem, vmem, vmem],
        out_specs=(vmem, pl.BlockSpec(memory_space=pl.ANY)),
        scratch_shapes=[pltpu.SemaphoreType.DMA]
        + [pltpu.VMEM((rows, 128), F32)] * 2 + [pltpu.VMEM((total + 16, channels), F32)] * 4,
        compiler_params=pltpu.CompilerParams(vmem_limit_bytes=57 * MIB),
        name="tail",
    )(arrived, visibilities, synth_taps, high, low)


def local(voltages, filter_taps, synth_taps, beam_weights, station_order):
    quarters, owners = lax.axis_size("beam"), lax.axis_size("stn")
    channels = filter_taps.shape[1]
    spectra = voltages.shape[2] // channels
    visibilities, arrived = main(voltages, beam_weights, filter_taps, station_order)
    series, visibilities = tail(arrived.reshape(-1, spectra), visibilities, synth_taps, quarters, owners)
    series = series.reshape(2, quarters * spectra, 2, channels).transpose(0, 2, 1, 3)
    return visibilities, series.reshape(2, 1, 2, quarters * spectra * channels)


def solution(mesh):
    in_specs = (P(None, "stn", "beam"), P(), P(), P(None, "stn", "beam", None), P())
    out_specs = (P(None, "stn", "beam", None), P(None, "beam", "stn", None))
    return jax.shard_map(local, mesh=mesh, in_specs=in_specs, out_specs=out_specs, check_vma=False)
```

time: 139 us -> 250 us (1.80)
  the two profiles are of different devices: /device:TPU:6 before, /device:TPU:1 now
where the time goes in v5:
time: 250 us; the launch traced here: 249 us
  Pallas kernels  249 us (100%)
    pallas_call x1, Pallas kernels, tail(): pl.pallas_call(functools.partial(tail_kernel, taps, quarters), out_shape=...  131 us
    pallas_call x1, Pallas kernels, main(): pl.pallas_call(functools.partial(main_kernel, quarters // 2, across * acr...  118 us

profile of v5, /device:TPU:1, one launch (start us, length us, event | category | flops | bytes accessed | tf_op | source)
XLA Modules:
  0.0 249.4 jit_solution(1137068338008443548)
XLA Ops:
  0.6 117.8 %main.1 = (f32[2,2,256,1024]{3,2,1,0:T(8,128)}, bf16[2,64,16,256]{3,2,1,0:T(8,128)(2,1)}) custom-call(bf16[2,16,32768]{2,1,0:T(8,128)(2,1)} %v_hbm.1, bf16[2,2,128,1024]{3,2,1,0:T(8,128)(2,1)} %w_hbm.1, f32[12,128]{1,0:T(8,128)} %taps_hbm.1, bf16[256,256]{1,0:T(8,128)(2,1)} %constant.8.clone.high_hbm, bf16[256,256]{1,0:T(8,128)(2,1)} %constant.9.clone.low_hbm, ...), custom_call_target="tpu_custom_call" | custom-call | tf_op jit(solution)/shard_map/main/pallas_call | solution.py:294
  118.5 130.8 %tail.1 = (f32[2,2048,128]{2,1,0:T(8,128)}, f32[2,2,256,1024]{3,2,1,0:T(8,128)}) custom-call(bf16[2048,256]{1,0:T(8,128)(2,1)} %bitcast.7, f32[2,2,256,1024]{3,2,1,0:T(8,128)} %get-tuple-element.7.vis_ref, f32[12,128]{1,0:T(8,128)} %taps_ref.1, bf16[256,256]{1,0:T(8,128)(2,1)} %constant.10.clone.high_ref, bf16[256,256]{1,0:T(8,128)(2,1)} %constant.11.clone.low_ref), custom_call_target="tpu_custom_call" | custom-call | tf_op jit(solution)/shard_map/tail/pallas_call | solution.py:374

commit v6 on v5

--- a/solution.py
+++ b/solution.py
@@ -326,10 +326,11 @@
 
 
 def tail_kernel(
-    taps, quarters, g_ref, vis_ref, taps_ref, high_ref, low_ref, out_ref, kept_ref, saved, left_ref, right_ref, *lines
+    taps, quarters, g_ref, vis_ref, taps_ref, high_ref, low_ref, out_ref, kept_ref, held_ref, saved, left_ref, right_ref, *lines
 ):
-    save = pltpu.make_async_copy(vis_ref, kept_ref, saved)
-    save.start()
+    fetch = pltpu.make_async_copy(vis_ref, held_ref, saved.at[0])
+    save = pltpu.make_async_copy(held_ref, kept_ref, saved.at[1])
+    fetch.start()
     channels = high_ref.shape[0] // 2
     spectra = g_ref.shape[1]
     pad = 16
@@ -351,6 +352,8 @@
             at = slice(pad + q * spectra, pad + (q + 1) * spectra)
             lines[2 * j][at, :] = result[:, :channels]
             lines[2 * j + 1][at, :] = result[:, channels:]
+    fetch.wait()
+    save.start()
     block = 64
     weights = [jnp.broadcast_to(taps_ref[m : m + 1, :], (block, channels)) for m in range(taps)]
     for j in range(2):
@@ -379,7 +382,7 @@
         ),
         in_specs=[vmem, pl.BlockSpec(memory_space=pl.ANY), vmem, vmem, vmem],
         out_specs=(vmem, pl.BlockSpec(memory_space=pl.ANY)),
-        scratch_shapes=[pltpu.SemaphoreType.DMA]
+        scratch_shapes=[pltpu.VMEM(visibilities.shape, F32), pltpu.SemaphoreType.DMA((2,))]
         + [pltpu.VMEM((rows, 128), F32)] * 2 + [pltpu.VMEM((total + 16, channels), F32)] * 4,
         compiler_params=pltpu.CompilerParams(vmem_limit_bytes=57 * MIB),
         name="tail",

time: 250 us -> 126 us (0.50)
  Pallas kernels: 249 us -> 125 us
    pallas_call x1, Pallas kernels: 131 us -> 6.82 us  [tail(): pl.pallas_call(functools.partial(tail_kernel, taps, quarters), out_shape=...]
where the time goes in v6:
time: 126 us; the launch traced here: 125 us
  Pallas kernels  125 us (99%)
    pallas_call x1, Pallas kernels, main(): pl.pallas_call(functools.partial(main_kernel, quarters // 2, across * acr...  118 us
    pallas_call x1, Pallas kernels, tail(): pl.pallas_call(functools.partial(tail_kernel, taps, quarters), out_shape=...  6.82 us

profile of v6, /device:TPU:1, one launch (start us, length us, event | category | flops | bytes accessed | tf_op | source)
XLA Modules:
  0.0 125.4 jit_solution(9437738257326669256)
XLA Ops:
  0.6 117.8 %main.1 = (f32[2,2,256,1024]{3,2,1,0:T(8,128)}, bf16[2,64,16,256]{3,2,1,0:T(8,128)(2,1)}) custom-call(bf16[2,16,32768]{2,1,0:T(8,128)(2,1)} %v_hbm.1, bf16[2,2,128,1024]{3,2,1,0:T(8,128)(2,1)} %w_hbm.1, f32[12,128]{1,0:T(8,128)} %taps_hbm.1, bf16[256,256]{1,0:T(8,128)(2,1)} %constant.8.clone.high_hbm, bf16[256,256]{1,0:T(8,128)(2,1)} %constant.9.clone.low_hbm, ...), custom_call_target="tpu_custom_call" | custom-call | tf_op jit(solution)/shard_map/main/pallas_call | solution.py:294
  118.5 6.8 %tail.1 = (f32[2,2048,128]{2,1,0:T(8,128)}, f32[2,2,256,1024]{3,2,1,0:T(8,128)}) custom-call(bf16[2048,256]{1,0:T(8,128)(2,1)} %bitcast.7, f32[2,2,256,1024]{3,2,1,0:T(8,128)} %get-tuple-element.7.vis_ref, f32[12,128]{1,0:T(8,128)} %taps_ref.1, bf16[256,256]{1,0:T(8,128)(2,1)} %constant.10.clone.high_ref, bf16[256,256]{1,0:T(8,128)(2,1)} %constant.11.clone.low_ref), custom_call_target="tpu_custom_call" | custom-call | tf_op jit(solution)/shard_map/tail/pallas_call | solution.py:377

commit v7 on v5

--- a/solution.py
+++ b/solution.py
@@ -71,7 +71,7 @@
     p, place = stn // planes, stn % planes
     x, y = place // across, place % across
     side, core = beam // 2, beam % 2
-    quarters, channels, _, stations, spectra = x_ref.shape
+    channels, quarters, _, stations, spectra = x_ref.shape
     rows = s_ref.shape[3]
     taps, points = taps_ref.shape
     mine, others = side * 2 + core, (1 - side) * 2 + core
@@ -150,48 +150,43 @@
         left_ref[pl.ds(i, lines, stride=rows), :] = result[:, :128]
         right_ref[pl.ds(i, lines, stride=rows), :] = result[:, 128:]
 
-    @pl.loop(0, owners // 4)
-    def _(i):
-        count = channels * 2 * rows
-        for j in range(4):
-            at = pl.ds(pl.multiple_of((i * 4 + j) * count, count), count)
-            s_ref[i * 4 + j, :, :, :, :128] = left_ref[at, :].astype(BF16).reshape(channels, 2, rows, 128)
-            s_ref[i * 4 + j, :, :, :, 128:] = right_ref[at, :].astype(BF16).reshape(channels, 2, rows, 128)
-
-    def entering(at, dx, groups):
+    def settle(c):
+        @pl.loop(0, owners // 8)
+        def _(i):
+            count = 2 * rows
+            for j in range(8):
+                at = pl.ds(pl.multiple_of((c * owners + i * 8 + j) * count, count), count)
+                s_ref[c, i * 8 + j, :, :, :128] = left_ref[at, :].astype(BF16).reshape(2, rows, 128)
+                s_ref[c, i * 8 + j, :, :, 128:] = right_ref[at, :].astype(BF16).reshape(2, rows, 128)
+
+    def entering(c, at, dx, groups):
         border = (p + 3 + 2 * at) % pairs_count
         for group in groups:
             pair, start = ((p, at), (border, at), (border, 1 - at), (far, 1 - at))[group]
             first = pl.multiple_of((pair * planes + ((x + across - dx) % across) * across) * rows, across * rows)
-            yield group, x_ref.at[start * 2 + core, :, :, pl.ds(first, across * rows), :], start
-
-    landing = x_ref.at[mine, :, :, pl.ds(pl.multiple_of(stn * rows, rows), rows), :]
-    pltpu.make_async_copy(s_ref.at[stn], landing, arrive.at[0, 0]).start()
-
-    def depart(group, dx, dy):
+            yield group, x_ref.at[c, start * 2 + core, :, pl.ds(first, across * rows), :], start
+
+    def landing(c):
+        return x_ref.at[c, mine, :, pl.ds(pl.multiple_of(stn * rows, rows), rows), :]
+
+    def stay(c):
+        pltpu.make_async_copy(s_ref.at[c, stn], landing(c), arrive.at[c, 0, 0]).start()
+
+    def depart(c, group, dx, dy):
         pair, entry = ((p, mine), (beyond, mine), (near, others), (far, others))[group]
         owner = pair * planes + ((x + dx) % across) * across + (y + dy) % across
-        remote(s_ref.at[owner], landing, send, arrive.at[group, dx], (owner, entry)).start()
-
-    @pl.loop(1, planes)
-    def _(i):
-        depart(0, i // across, i % across)
-
-    @pl.loop(0, planes)
-    def _(i):
-        for group in (3, 1, 2):
-            depart(group, i // across, i % across)
-
-    def entered(groups, dx):
-        for group, block, start in entering(side, dx, groups):
-            wait(block, arrive.at[group, dx])
-            remote(block, block, forward, forwarded.at[group, dx], partner).start()
-            remote(block, block, share.at[start], shared.at[start], sibling).start()
-
-    def passed(groups, dx):
-        for group, block, start in entering(1 - side, dx, groups):
-            wait(block, forwarded.at[group, dx])
-            remote(block, block, share.at[start], shared.at[start], sibling).start()
+        remote(s_ref.at[c, owner], landing(c), send.at[c], arrive.at[c, group, dx], (owner, entry)).start()
+
+    def entered(c, groups, dx):
+        for group, block, start in entering(c, side, dx, groups):
+            wait(block, arrive.at[c, group, dx])
+            remote(block, block, forward.at[c], forwarded.at[c, group, dx], partner).start()
+            remote(block, block, share.at[c, start], shared.at[c, start], sibling).start()
+
+    def passed(c, groups, dx):
+        for group, block, start in entering(c, 1 - side, dx, groups):
+            wait(block, forwarded.at[c, group, dx])
+            remote(block, block, share.at[c, start], shared.at[c, start], sibling).start()
 
     half = w_ref.shape[2]
 
@@ -203,40 +198,18 @@
             crossed = jnp.concatenate([-turned[half:], turned[:half]], axis=0)
             weights_ref[c, :, stations + at : stations + at + 256] = crossed.astype(BF16)
 
-    @pl.loop(0, across)
-    def _(dx):
-        entered((0,), dx)
-
-    fetches[4].wait()
-
-    @pl.loop(0, across)
-    def _(step):
-        entered((2, 1, 3), step)
-
-        @pl.when(step < channels)
-        def _():
-            weigh(step)
-
-        passed((0,), step)
-
-        @pl.when(step > 0)
-        def _():
-            passed((2, 1, 3), step - 1)
-
-    passed((2, 1, 3), across - 1)
-    for start in range(sides):
-        wait(x_ref.at[start * 2 + 1 - core], shared.at[start])
-
-    @pl.loop(0, channels)
-    def _(c):
+    def beams(c):
+        for start in range(sides):
+            wait(x_ref.at[c, start * 2 + 1 - core], shared.at[c, start])
+
         @pl.loop(0, quarters)
         def _(q):
-            result = dot(weights_ref[c, :, :stations], x_ref[q, c, 0], nn)
-            result += dot(weights_ref[c, :, stations:], x_ref[q, c, 1], nn)
+            result = dot(weights_ref[c, :, :stations], x_ref[c, q, 0], nn)
+            result += dot(weights_ref[c, :, stations:], x_ref[c, q, 1], nn)
             for part in range(2):
-                beams = result[part * half : (part + 1) * half]
-                left_ref[pl.ds(q * 2 + part, half, stride=8), :] = beams[:, :128]
-                right_ref[pl.ds(q * 2 + part, half, stride=8), :] = beams[:, 128:]
+                formed = result[part * half : (part + 1) * half]
+                left_ref[pl.ds(q * 2 + part, half, stride=8), :] = formed[:, :128]
+                right_ref[pl.ds(q * 2 + part, half, stride=8), :] = formed[:, 128:]
 
         for d in range(0, owners, 8):
             at = slice(d * 16, (d + 8) * 16)
@@ -245,24 +218,32 @@
 
         pltpu.make_async_copy(formed_ref.at[c, stn], got_ref.at[c, stn], beam_arrive.at[c]).start()
 
-        @pl.loop(1, owners)
+        def dispatch(owner):
+            remote(formed_ref.at[c, owner], got_ref.at[c, stn], beam_send.at[c], beam_arrive.at[c], (owner, beam)).start()
+
+        @pl.loop(0, planes)
         def _(i):
-            owner = (stn + i) % owners
-            remote(formed_ref.at[c, owner], got_ref.at[c, stn], beam_send.at[c], beam_arrive.at[c], (owner, beam)).start()
+            for pair in (far, near, beyond):
+                dispatch(pair * planes + (place + i) % planes)
+
+            @pl.when(i > 0)
+            def _():
+                dispatch(p * planes + (place + i) % planes)
 
     count = vis_ref.shape[2]
-    start = pl.multiple_of(beam * count, count)
+    first_row = pl.multiple_of(beam * count, count)
     scale = 1.0 / (quarters * spectra)
 
-    @pl.loop(0, channels)
-    def _(c):
-        for q in range(quarters):
+    def arrange(c, some):
+        for q in some:
             at = slice(q * spectra, (q + 1) * spectra)
             for part in range(2):
                 for r in range(0, stations, 256):
-                    turned_ref[part, r : r + 256, at] = dot(pick_ref[r : r + 256, :], x_ref[q, c, part], nn).astype(BF16)
-        real_rows = turned_ref[0, pl.ds(start, count), :]
-        imag_rows = turned_ref[1, pl.ds(start, count), :]
+                    turned_ref[part, r : r + 256, at] = dot(pick_ref[r : r + 256, :], x_ref[c, q, part], nn).astype(BF16)
+
+    def correlate(c):
+        real_rows = turned_ref[0, pl.ds(first_row, count), :]
+        imag_rows = turned_ref[1, pl.ds(first_row, count), :]
         for at in range(0, stations, 256):
             cols = slice(at, at + 256)
             real, imag = turned_ref[0, cols, :], turned_ref[1, cols, :]
@@ -270,15 +251,86 @@
             vis_ref[1, c, :, cols] = (dot(imag_rows, real, nt) - dot(real_rows, imag, nt)) * scale
         pltpu.make_async_copy(vis_ref.at[:, c], vis_hbm.at[:, c], saves.at[c]).start()
 
-    for start in range(sides):
-        wait(x_ref.at[start * 2 + core], share.at[start])
-    wait(x_ref.at[0], forward)
-    wait(s_ref.at[pl.ds(0, owners - 1)], send)
+    outer = (2, 1, 3)
+    last = across - 1
+    settle(0)
+    stay(0)
+
+    @pl.loop(1, planes)
+    def _(i):
+        depart(0, 0, i // across, i % across)
+
+    @pl.loop(0, planes)
+    def _(i):
+        for group in (3, 1, 2):
+            depart(0, group, i // across, i % across)
+
+    settle(1)
+
+    @pl.loop(0, across)
+    def _(dx):
+        entered(0, (0,), dx)
+
+    fetches[4].wait()
+    stay(1)
+
+    @pl.loop(0, across)
+    def _(step):
+        entered(0, outer, step)
+
+        @pl.loop(0, across)
+        def _(dy):
+            @pl.when((step > 0) | (dy > 0))
+            def _():
+                depart(1, 0, step, dy)
+
+            for group in (3, 1, 2):
+                depart(1, group, step, dy)
+
+        @pl.when(step < channels)
+        def _():
+            weigh(step)
+
+        passed(0, (0,), step)
+
+        @pl.when(step > 0)
+        def _():
+            passed(0, outer, step - 1)
+
+    @pl.loop(0, across)
+    def _(dx):
+        entered(1, (0,), dx)
+
+    passed(0, outer, last)
+    beams(0)
+    entered(1, outer, 0)
+    passed(1, (0,), 0)
+    arrange(0, (0, 1))
+    entered(1, outer, 1)
+    passed(1, (0,), 1)
+    passed(1, outer, 0)
+    arrange(0, (2, 3))
+    entered(1, outer, 2)
+    passed(1, (0,), 2)
+    passed(1, outer, 1)
+    correlate(0)
+    entered(1, outer, 3)
+    passed(1, (0,), 3)
+    passed(1, outer, 2)
+    passed(1, outer, 3)
+    beams(1)
+    arrange(1, range(quarters))
+    correlate(1)
+
     wait(rim_ref, rim_send)
     for c in range(channels):
+        for start in range(sides):
+            wait(x_ref.at[c, start * 2 + core], share.at[c, start])
+        wait(x_ref.at[c, 0], forward.at[c])
+        wait(s_ref.at[c, pl.ds(0, owners - 1)], send.at[c])
+        wait(formed_ref.at[c, pl.ds(0, owners - 1)], beam_send.at[c])
         wait(vis_ref.at[:, c], saves.at[c])
         wait(got_ref.at[c], beam_arrive.at[c])
-        wait(formed_ref.at[c, pl.ds(0, owners - 1)], beam_send.at[c])
 
 
 def main(voltages, beam_weights, filter_taps, station_order):
@@ -287,7 +339,7 @@
     rows, spectra = voltages.shape[1], voltages.shape[2] // points
     channels, half, stations = beam_weights.shape[1:]
     across = 4
-    order = np.array([ri * points + c for c in range(points) for ri in range(2)])
+    order = np.arange(2 * points).reshape(2, owners, channels).transpose(2, 1, 0).reshape(-1)
     high, low = split(spin_matrix(points).T[order])
     dma = pltpu.SemaphoreType.DMA
     vmem, anywhere = pl.BlockSpec(memory_space=pltpu.VMEM), pl.BlockSpec(memory_space=pl.ANY)
@@ -310,14 +362,16 @@
             pltpu.VMEM((spectra * rows, points), F32),
             pltpu.VMEM((2 * points * rows, 128), F32),
             pltpu.VMEM((2 * points * rows, 128), F32),
-            pltpu.VMEM((owners, channels, 2, rows, spectra), BF16),
-            pltpu.VMEM((quarters, channels, 2, stations, spectra), BF16),
+            pltpu.VMEM((channels, owners, 2, rows, spectra), BF16),
+            pltpu.VMEM((channels, quarters, 2, stations, spectra), BF16),
             pltpu.VMEM((channels, 2 * half, 2 * stations), BF16),
             pltpu.VMEM((stations, stations), BF16),
             pltpu.VMEM((channels, owners, 16, spectra), BF16),
             pltpu.VMEM((2, stations, quarters * spectra), BF16),
             pltpu.VMEM((2, channels, stations // quarters, stations), F32),
-            dma((5,)), dma((channels,)), dma, dma, dma, dma((4, across)), dma, dma((4, across)), dma((2,)), dma((2,)),
+            dma((5,)), dma((channels,)), dma, dma,
+            dma((channels,)), dma((channels, 4, across)), dma((channels,)), dma((channels, 4, across)),
+            dma((channels, 2)), dma((channels, 2)),
             dma((channels,)), dma((channels,)),
         ],
         compiler_params=pltpu.CompilerParams(collective_id=0, has_side_effects=True, vmem_limit_bytes=54 * MIB),
@@ -326,10 +380,13 @@
 
 
 def tail_kernel(
-    taps, quarters, g_ref, vis_ref, taps_ref, high_ref, low_ref, out_ref, kept_ref, saved, left_ref, right_ref, *lines
+    taps, quarters, g_ref, vis_ref, taps_ref, high_ref, low_ref, out_ref, kept_ref, held_ref, saved, left_ref, right_ref, *lines
 ):
-    save = pltpu.make_async_copy(vis_ref, kept_ref, saved)
-    save.start()
+    pieces = [(i, c) for i in range(2) for c in range(vis_ref.shape[1])]
+    fetches = [pltpu.make_async_copy(vis_ref.at[i], held_ref.at[i], saved.at[0, n]) for n, i in enumerate(pieces)]
+    saves = [pltpu.make_async_copy(held_ref.at[i], kept_ref.at[i], saved.at[1, n]) for n, i in enumerate(pieces)]
+    for fetch in fetches:
+        fetch.start()
     channels = high_ref.shape[0] // 2
     spectra = g_ref.shape[1]
     pad = 16
@@ -351,6 +408,9 @@
             at = slice(pad + q * spectra, pad + (q + 1) * spectra)
             lines[2 * j][at, :] = result[:, :channels]
             lines[2 * j + 1][at, :] = result[:, channels:]
+    for fetch, save in zip(fetches, saves):
+        fetch.wait()
+        save.start()
     block = 64
     weights = [jnp.broadcast_to(taps_ref[m : m + 1, :], (block, channels)) for m in range(taps)]
     for j in range(2):
@@ -361,7 +421,8 @@
                 for m in range(1, taps):
                     total += weights[m] * line[pad + t - m : pad + t - m + block, :]
                 out_ref[part, pl.ds(2 * t + j, block, stride=2), :] = total
-    save.wait()
+    for save in saves:
+        save.wait()
 
 
 def tail(arrived, visibilities, synth_taps, quarters, owners):
@@ -379,7 +440,7 @@
         ),
         in_specs=[vmem, pl.BlockSpec(memory_space=pl.ANY), vmem, vmem, vmem],
         out_specs=(vmem, pl.BlockSpec(memory_space=pl.ANY)),
-        scratch_shapes=[pltpu.SemaphoreType.DMA]
+        scratch_shapes=[pltpu.VMEM(visibilities.shape, F32), pltpu.SemaphoreType.DMA((2, 4))]
         + [pltpu.VMEM((rows, 128), F32)] * 2 + [pltpu.VMEM((total + 16, channels), F32)] * 4,
         compiler_params=pltpu.CompilerParams(vmem_limit_bytes=57 * MIB),
         name="tail",

time: 250 us -> 126 us (0.50)
  Pallas kernels: 249 us -> 125 us
    pallas_call x1, Pallas kernels: 131 us -> 6.45 us  [tail(): pl.pallas_call(functools.partial(tail_kernel, taps, quarters), out_shape=...]
where the time goes in v7:
time: 126 us
  Pallas kernels  125 us (99%)
    pallas_call x1, Pallas kernels, main(): pl.pallas_call(functools.partial(main_kernel, quarters // 2, across * acr...  118 us
    pallas_call x1, Pallas kernels, tail(): pl.pallas_call(functools.partial(tail_kernel, taps, quarters), out_shape=...  6.45 us

profile of v7, /device:TPU:1, one launch (start us, length us, event | category | flops | bytes accessed | tf_op | source)
XLA Modules:
  0.0 125.6 jit_solution(7757272314932808598)
XLA Ops:
  0.6 118.3 %main.1 = (f32[2,2,256,1024]{3,2,1,0:T(8,128)}, bf16[2,64,16,256]{3,2,1,0:T(8,128)(2,1)}) custom-call(bf16[2,16,32768]{2,1,0:T(8,128)(2,1)} %v_hbm.1, bf16[2,2,128,1024]{3,2,1,0:T(8,128)(2,1)} %w_hbm.1, f32[12,128]{1,0:T(8,128)} %taps_hbm.1, bf16[256,256]{1,0:T(8,128)(2,1)} %constant.8.clone.high_hbm, bf16[256,256]{1,0:T(8,128)(2,1)} %constant.9.clone.low_hbm, ...), custom_call_target="tpu_custom_call" | custom-call | tf_op jit(solution)/shard_map/main/pallas_call | solution.py:346
  119.0 6.5 %tail.1 = (f32[2,2048,128]{2,1,0:T(8,128)}, f32[2,2,256,1024]{3,2,1,0:T(8,128)}) custom-call(bf16[2048,256]{1,0:T(8,128)(2,1)} %bitcast.7, f32[2,2,256,1024]{3,2,1,0:T(8,128)} %get-tuple-element.7.vis_ref, f32[12,128]{1,0:T(8,128)} %taps_ref.1, bf16[256,256]{1,0:T(8,128)(2,1)} %constant.10.clone.high_ref, bf16[256,256]{1,0:T(8,128)(2,1)} %constant.11.clone.low_ref), custom_call_target="tpu_custom_call" | custom-call | tf_op jit(solution)/shard_map/tail/pallas_call | solution.py:435

commit v8 on v7

--- a/solution.py
+++ b/solution.py
@@ -105,25 +105,23 @@
     filters = [jnp.broadcast_to(taps_ref[m : m + 1, :], (rows, points)) for m in range(taps)]
     stores = (re_ref, im_ref)
 
-    @pl.loop(2, spectra // 8)
-    def _(block):
-        for part in range(2):
-
-            def tile(i, part=part):
-                return v_ref[part, :, pl.ds(pl.multiple_of((block * 8 + i) * points, points), points)].astype(F32)
-
-            fir(taps, tile, filters, block * 8, stores[part])
-
+    def inner(first, end):
+        @pl.loop(first, end)
+        def _(block):
+            for part in range(2):
+
+                def tile(i, part=part):
+                    return v_ref[part, :, pl.ds(pl.multiple_of((block * 8 + i) * points, points), points)].astype(F32)
+
+                fir(taps, tile, filters, block * 8, stores[part])
+
+    blocks = spectra // 8
+    inner(2, blocks // 2)
     pl.semaphore_wait(pltpu.get_barrier_semaphore(), owners - 1 + 2 * planes + 3)
     rim = (taps - 1) * points
     remote(v_ref.at[:, :, pl.ds((spectra - taps + 1) * points, rim)], rim_ref, rim_send, rim_arrive, later).start()
 
-    @pl.loop(0, stations // 64)
-    def _(i):
-        first = pl.multiple_of(i * 64, 64)
-        station = lax.broadcasted_iota(jnp.int32, (64, stations), 0) + first
-        pick_ref[pl.ds(first, 64), :] = jnp.where(order_ref[...] == station, 1.0, 0.0).astype(BF16)
-
+    inner(blocks // 2, blocks)
     wait(rim_ref, rim_arrive)
     for block in range(2):
         for part in range(2):
@@ -140,15 +138,17 @@
 
     fetches[2].wait()
     fetches[3].wait()
-    lines = 2 * points
-    for i in range(rows):
-        at = pl.ds(i, spectra, stride=rows)
-        wide = jnp.concatenate([re_ref[at, :], im_ref[at, :]], axis=1)
-        high = wide.astype(BF16)
-        low = (wide - high.astype(F32)).astype(BF16)
-        result = dot(high_ref[...], high, nt) + dot(high_ref[...], low, nt) + dot(low_ref[...], high, nt)
-        left_ref[pl.ds(i, lines, stride=rows), :] = result[:, :128]
-        right_ref[pl.ds(i, lines, stride=rows), :] = result[:, 128:]
+    def transform(c):
+        lines = 2 * owners
+        cut = slice(c * lines, (c + 1) * lines)
+        for i in range(rows):
+            at = pl.ds(i, spectra, stride=rows)
+            wide = jnp.concatenate([re_ref[at, :], im_ref[at, :]], axis=1)
+            high = wide.astype(BF16)
+            low = (wide - high.astype(F32)).astype(BF16)
+            result = dot(high_ref[cut, :], high, nt) + dot(high_ref[cut, :], low, nt) + dot(low_ref[cut, :], high, nt)
+            left_ref[pl.ds(c * lines * rows + i, lines, stride=rows), :] = result[:, :128]
+            right_ref[pl.ds(c * lines * rows + i, lines, stride=rows), :] = result[:, 128:]
 
     def settle(c):
         @pl.loop(0, owners // 8)
@@ -253,6 +253,7 @@
 
     outer = (2, 1, 3)
     last = across - 1
+    transform(0)
     settle(0)
     stay(0)
 
@@ -265,11 +266,18 @@
         for group in (3, 1, 2):
             depart(0, group, i // across, i % across)
 
+    transform(1)
     settle(1)
 
     @pl.loop(0, across)
     def _(dx):
         entered(0, (0,), dx)
+
+    @pl.loop(0, stations // 64)
+    def _(i):
+        first = pl.multiple_of(i * 64, 64)
+        station = lax.broadcasted_iota(jnp.int32, (64, stations), 0) + first
+        pick_ref[pl.ds(first, 64), :] = jnp.where(order_ref[...] == station, 1.0, 0.0).astype(BF16)
 
     fetches[4].wait()
     stay(1)

time: 126 us -> 125 us (level)
  no operation moved by 1% of the time
where the time goes in v8:
time: 125 us
  Pallas kernels  124 us (99%)
    pallas_call x1, Pallas kernels, main(): pl.pallas_call(functools.partial(main_kernel, quarters // 2, across * acr...  118 us
    pallas_call x1, Pallas kernels, tail(): pl.pallas_call(functools.partial(tail_kernel, taps, quarters), out_shape=...  6.45 us

profile of v8, /device:TPU:1, one launch (start us, length us, event | category | flops | bytes accessed | tf_op | source)
XLA Modules:
  0.0 125.0 jit_solution(8539325993984577404)
XLA Ops:
  0.6 117.7 %main.1 = (f32[2,2,256,1024]{3,2,1,0:T(8,128)}, bf16[2,64,16,256]{3,2,1,0:T(8,128)(2,1)}) custom-call(bf16[2,16,32768]{2,1,0:T(8,128)(2,1)} %v_hbm.1, bf16[2,2,128,1024]{3,2,1,0:T(8,128)(2,1)} %w_hbm.1, f32[12,128]{1,0:T(8,128)} %taps_hbm.1, bf16[256,256]{1,0:T(8,128)(2,1)} %constant.8.clone.high_hbm, bf16[256,256]{1,0:T(8,128)(2,1)} %constant.9.clone.low_hbm, ...), custom_call_target="tpu_custom_call" | custom-call | tf_op jit(solution)/shard_map/main/pallas_call | solution.py:354
  118.3 6.5 %tail.1 = (f32[2,2048,128]{2,1,0:T(8,128)}, f32[2,2,256,1024]{3,2,1,0:T(8,128)}) custom-call(bf16[2048,256]{1,0:T(8,128)(2,1)} %bitcast.7, f32[2,2,256,1024]{3,2,1,0:T(8,128)} %get-tuple-element.7.vis_ref, f32[12,128]{1,0:T(8,128)} %taps_ref.1, bf16[256,256]{1,0:T(8,128)(2,1)} %constant.10.clone.high_ref, bf16[256,256]{1,0:T(8,128)(2,1)} %constant.11.clone.low_ref), custom_call_target="tpu_custom_call" | custom-call | tf_op jit(solution)/shard_map/tail/pallas_call | solution.py:443

commit v9 on v8

--- a/solution.py
+++ b/solution.py
@@ -268,6 +268,19 @@
 
     transform(1)
     settle(1)
+    stay(1)
+
+    def follow(dx):
+        @pl.loop(0, across)
+        def _(dy):
+            for group in (3, 1, 2):
+                depart(1, group, dx, dy)
+
+    @pl.loop(1, planes)
+    def _(i):
+        depart(1, 0, i // across, i % across)
+
+    follow(0)
 
     @pl.loop(0, across)
     def _(dx):
@@ -280,20 +293,14 @@
         pick_ref[pl.ds(first, 64), :] = jnp.where(order_ref[...] == station, 1.0, 0.0).astype(BF16)
 
     fetches[4].wait()
-    stay(1)
 
     @pl.loop(0, across)
     def _(step):
         entered(0, outer, step)
 
-        @pl.loop(0, across)
-        def _(dy):
-            @pl.when((step > 0) | (dy > 0))
-            def _():
-                depart(1, 0, step, dy)
-
-            for group in (3, 1, 2):
-                depart(1, group, step, dy)
+        @pl.when(step < last)
+        def _():
+            follow(step + 1)
 
         @pl.when(step < channels)
         def _():
@@ -388,7 +395,7 @@
 
 
 def tail_kernel(
-    taps, quarters, g_ref, vis_ref, taps_ref, high_ref, low_ref, out_ref, kept_ref, held_ref, saved, left_ref, right_ref, *lines
+    taps, quarters, g_ref, vis_ref, taps_ref, high_ref, low_ref, out_hbm, kept_ref, held_ref, saved, out_ref, left_ref, right_ref, *lines
 ):
     pieces = [(i, c) for i in range(2) for c in range(vis_ref.shape[1])]
     fetches = [pltpu.make_async_copy(vis_ref.at[i], held_ref.at[i], saved.at[0, n]) for n, i in enumerate(pieces)]
@@ -421,14 +428,18 @@
         save.start()
     block = 64
     weights = [jnp.broadcast_to(taps_ref[m : m + 1, :], (block, channels)) for m in range(taps)]
-    for j in range(2):
-        for part in range(2):
+    leaving = [pltpu.make_async_copy(out_ref.at[part], out_hbm.at[part], saved.at[part, len(pieces)]) for part in range(2)]
+    for part in range(2):
+        for j in range(2):
             line = lines[2 * j + part]
             for t in range(0, quarters * spectra, block):
                 total = weights[0] * line[pad + t : pad + t + block, :]
                 for m in range(1, taps):
                     total += weights[m] * line[pad + t - m : pad + t - m + block, :]
                 out_ref[part, pl.ds(2 * t + j, block, stride=2), :] = total
+        leaving[part].start()
+    for leave in leaving:
+        leave.wait()
     for save in saves:
         save.wait()
 
@@ -447,8 +458,8 @@
             jax.ShapeDtypeStruct(visibilities.shape, F32),
         ),
         in_specs=[vmem, pl.BlockSpec(memory_space=pl.ANY), vmem, vmem, vmem],
-        out_specs=(vmem, pl.BlockSpec(memory_space=pl.ANY)),
-        scratch_shapes=[pltpu.VMEM(visibilities.shape, F32), pltpu.SemaphoreType.DMA((2, 4))]
+        out_specs=(pl.BlockSpec(memory_space=pl.ANY),) * 2,
+        scratch_shapes=[pltpu.VMEM(visibilities.shape, F32), pltpu.SemaphoreType.DMA((2, 5)), pltpu.VMEM((2, 2 * total, channels), F32)]
         + [pltpu.VMEM((rows, 128), F32)] * 2 + [pltpu.VMEM((total + 16, channels), F32)] * 4,
         compiler_params=pltpu.CompilerParams(vmem_limit_bytes=57 * MIB),
         name="tail",

time: 125 us -> 126 us (level)
  no operation moved by 1% of the time
where the time goes in v9:
time: 126 us
  Pallas kernels  125 us (99%)
    pallas_call x1, Pallas kernels, main(): pl.pallas_call(functools.partial(main_kernel, quarters // 2, across * acr...  119 us
    pallas_call x1, Pallas kernels, tail(): pl.pallas_call(functools.partial(tail_kernel, taps, quarters), out_shape=...  6.12 us

profile of v9, /device:TPU:1, one launch (start us, length us, event | category | flops | bytes accessed | tf_op | source)
XLA Modules:
  0.0 125.7 jit_solution(12583649763939412937)
XLA Ops:
  0.6 118.7 %main.1 = (f32[2,2,256,1024]{3,2,1,0:T(8,128)}, bf16[2,64,16,256]{3,2,1,0:T(8,128)(2,1)}) custom-call(bf16[2,16,32768]{2,1,0:T(8,128)(2,1)} %v_hbm.1, bf16[2,2,128,1024]{3,2,1,0:T(8,128)(2,1)} %w_hbm.1, f32[12,128]{1,0:T(8,128)} %taps_hbm.1, bf16[256,256]{1,0:T(8,128)(2,1)} %constant.8.clone.high_hbm, bf16[256,256]{1,0:T(8,128)(2,1)} %constant.9.clone.low_hbm, ...), custom_call_target="tpu_custom_call" | custom-call | tf_op jit(solution)/shard_map/main/pallas_call | solution.py:361
  119.3 6.1 %tail.1 = (f32[2,2048,128]{2,1,0:T(8,128)}, f32[2,2,256,1024]{3,2,1,0:T(8,128)}) custom-call(bf16[2048,256]{1,0:T(8,128)(2,1)} %bitcast.7, f32[2,2,256,1024]{3,2,1,0:T(8,128)} %get-tuple-element.7.vis_ref, f32[12,128]{1,0:T(8,128)} %taps_ref.1, bf16[256,256]{1,0:T(8,128)(2,1)} %constant.10.clone.high_ref, bf16[256,256]{1,0:T(8,128)(2,1)} %constant.11.clone.low_ref), custom_call_target="tpu_custom_call" | custom-call | tf_op jit(solution)/shard_map/tail/pallas_call | solution.py:454
